TPU v7x, 256 devices: a whole 4x4x8 slice. The times are simulated.
256 devices in a mesh: pts: 16 (over z, core), trc: 16 (over y, x).
Axes of the slice: x: 4, y: 4, z: 8, core: 2. Of those that a mesh axis runs over, the one named last changes fastest.
Arguments:
- tracers: float32 [64, 49152], P('trc', 'pts'), may hold values from -6 to 6
- explicit_blocks: bfloat16 [2, 384, 4, 128, 128], P(None, 'pts'), may hold values from -0.375 to 0.375
- implicit_blocks: bfloat16 [2, 384, 4, 128, 128], P(None, 'pts'), may hold values from -0.375 to 0.375
- column_blocks: int32 [384, 4], P('pts'), may hold values from 0 to 383, as said below
- block_count: int32 [384], P('pts'), may hold values from 1 to 4
- month_pair: int32 [2], replicated, may hold values from 0 to 1, as said below
- weight_num: int32 [2], replicated, may hold values from 0 to 30
- source_mix: float32 [64, 64], replicated, may hold values from -0.75 to 0.75
- source_bias: float32 [64], replicated, may hold values from -3 to 3
- source_rate: float32 [64], replicated, may hold values from 0.2 to 2
Outputs:
- advanced: float32 [64, 49152], P('trc', 'pts')
Inputs may be any that keep to these rules, and one draw needn't show every extreme that they name: `month_pair`: the two months differ. column_blocks[n, r] = (n + d) mod 384 with -2 <= d < 2, the entries of one row-block distinct.
All inputs are finite; a program needn't handle non-finite values.
Results may differ from a plain program's by a relative error of at most 0.0003.
Values sent between devices are 32-bit elements; how exact they have to be, the bound alone decides.
No kernel may reach another device: no remote copies, remote signals or barrier semaphores. Data moves between devices by JAX's collectives and lax.ppermute only.
A program may use at most 64 MiB of HBM per device.

v0:
```python
import jax
import jax.numpy as jnp
from jax import lax
from jax.sharding import PartitionSpec as P

REACH = 2
DAYS = 30
STEPS = 2


def extended(block, sides, width):
    for axis, dim in sides:
        count = lax.axis_size(axis)
        forward = [(i, i + 1) for i in range(count - 1)]
        forward.append((count - 1, 0))
        backward = [(target, source) for source, target in forward]
        low = lax.ppermute(
            lax.slice_in_dim(block, block.shape[dim] - width, None, axis=dim), axis, forward
        )
        high = lax.ppermute(lax.slice_in_dim(block, 0, width, axis=dim), axis, backward)
        block = jnp.concatenate([low, block, high], axis=dim)
    return block


def interpolate(blocks, month_pair, numer):
    first = lax.dynamic_index_in_dim(blocks, month_pair[0], 0, keepdims=False).astype(jnp.float32)
    second = lax.dynamic_index_in_dim(blocks, month_pair[1], 0, keepdims=False).astype(jnp.float32)
    weight = numer.astype(jnp.float32) / DAYS
    return (1.0 - weight) * first + weight * second


def apply_local(matrix, column_blocks, used, whole):
    rows_here = whole.shape[0]
    block_size = matrix.shape[-1]
    split = whole.reshape(rows_here, whole.shape[1] // block_size, block_size)
    picked = split[:, column_blocks] * used[None, :, :, None]
    out = jnp.einsum("nrij,tnrj->tni", matrix, picked, precision=lax.Precision.HIGHEST)
    return out.reshape(rows_here, matrix.shape[0] * block_size)


def source_terms(field, mixing, offset, rate):
    inner = jnp.dot(mixing, field, precision=lax.Precision.HIGHEST) + offset[:, None]
    return rate[:, None] * inner * jnp.exp(-0.125 * inner * inner)


def per_device(
    tracers,
    explicit_blocks,
    implicit_blocks,
    column_blocks,
    block_count,
    month_pair,
    weight_num,
    source_mix,
    source_bias,
    source_rate,
):
    width = column_blocks.shape[1]
    blocks_here = column_blocks.shape[0]
    block_size = explicit_blocks.shape[-1]
    total_blocks = blocks_here * lax.axis_size("pts")
    used = (jnp.arange(width)[None, :] < block_count[:, None]).astype(jnp.float32)
    local_cols = (column_blocks - lax.axis_index("pts") * blocks_here + REACH) % total_blocks
    field = tracers
    for step in range(STEPS):
        explicit_op = interpolate(explicit_blocks, month_pair, weight_num[step])
        implicit_op = interpolate(implicit_blocks, month_pair, weight_num[step])
        padded = extended(field, (("pts", 1),), REACH * block_size)
        middle = apply_local(explicit_op, local_cols, used, padded)
        grouped = lax.all_to_all(field, "trc", split_axis=1, concat_axis=0, tiled=True)
        terms = source_terms(grouped, source_mix, source_bias, source_rate)
        terms = lax.all_to_all(terms, "trc", split_axis=0, concat_axis=1, tiled=True)
        middle = middle + 0.5 * terms
        padded_mid = extended(middle, (("pts", 1),), REACH * block_size)
        field = apply_local(implicit_op, local_cols, used, padded_mid)
    return field


def solution(mesh):
    in_specs = (
        P("trc", "pts"),
        P(None, "pts", None, None, None),
        P(None, "pts", None, None, None),
        P("pts", None),
        P("pts"),
        P(),
        P(),
        P(),
        P(),
        P(),
    )
    out_specs = P("trc", "pts")
    return jax.shard_map(
        per_device, mesh=mesh, in_specs=in_specs, out_specs=out_specs, check_vma=False
    )
```

profile of v0, /device:TPU:16, one launch (start us, length us, event | category | flops | bytes accessed | tf_op | source)
XLA Modules:
  0.0 104.9 jit_solution(16327873481599793300)
XLA Ops:
  0.0 0.9 all_to_all.48
  0.9 0.7 copy.25
  1.6 7.3 %all-to-all-start = ((f32[4,16,192]{2,0,1:T(4,128)}), f32[4,16,192]{2,0,1:T(4,128)S(1)}, u32[]{:S(2)}, u32[]{:S(2)}) async-start(f32[4,16,192]{2,0,1:T(4,128)} %copy.25), calls=%async_computation | async-start | bytes 131072 | tf_op jit(solution)/shard_map/all_to_all | solution.py:70
  8.9 0.7 fusion.72
  9.6 4.7 %collective-permute-start.1 = (f32[4,256]{1,0:T(4,128)S(1)}, f32[4,256]{1,0:T(4,128)S(1)}, u32[]{:S(2)}, u32[]{:S(2)}) collective-permute-start(f32[4,256]{1,0:T(4,128)S(1)} %get-tuple-element.12), channel_id=1, source_target_pairs={{16,0},{32,16},{48,32},{64,48},{80,64},{96,80},{112,96},{128,112},... | collective-permute-start | bytes 12296 | tf_op jit(solution)/shard_map/ppermute | solution.py:20
  14.3 1.4 %fusion.73 = (s32[1]{0:T(128)}, s32[1]{0:T(128)}) fusion(s32[2]{0:T(128)} %param.16), kind=kLoop, calls=%fused_computation.86 | loop fusion | bytes 16 | tf_op jit(solution)/shard_map/slice | solution.py:66
  15.7 1.3 %fusion.74 = (s32[1]{0:T(128)}, s32[1]{0:T(128)}) fusion(s32[2]{0:T(128)} %param.15), kind=kLoop, calls=%fused_computation.87 | loop fusion | bytes 16 | tf_op jit(solution)/shard_map/slice | solution.py:26
  17.0 0.7 compare_select_fusion
  17.7 0.1 copy.23
  17.8 0.1 reshape.105
  17.9 0.7 fusion.64
  23.0 0.0 all-to-all-done
  23.1 0.9 fusion.61
  24.0 0.6 all_to_all.52
  24.6 7.2 %all-to-all-start.1 = ((f32[16,4,192]{2,1,0:T(4,128)}), f32[16,4,192]{2,1,0:T(4,128)S(1)}, u32[]{:S(2)}, u32[]{:S(2)}) async-start(f32[16,4,192]{2,1,0:T(4,128)} %all_to_all.52), calls=%async_computation.1 | async-start | bytes 131072 | tf_op jit(solution)/shard_map/all_to_all | solution.py:72
  31.9 0.0 collective-permute-done
  31.9 0.8 maximum_bitcast_fusion
  32.7 0.7 gather_fusion
  33.4 3.9 %all-to-all-done.1 = f32[16,4,192]{2,1,0:T(4,128)S(1)} async-done(((f32[16,4,192]{2,1,0:T(4,128)}), f32[16,4,192]{2,1,0:T(4,128)S(1)}, u32[]{:S(2)}, u32[]{:S(2)}) %all-to-all-start.1) | async-done | bytes 49184 | tf_op jit(solution)/shard_map/all_to_all | solution.py:72
  37.3 0.1 mul.141
  37.4 7.8 %fusion.25 = f32[4,3072]{1,0:T(4,128)S(1)} fusion(f32[4,3072]{1,0:T(4,128)S(1)} %mul.141, f32[]{:T(128)} %bitcast.3, f32[]{:T(128)S(6)} %sub.16, bf16[2,24,4,128,128]{4,3,2,1,0:T(8,128)(2,1)} %param.11, s32[]{:T(128)S(6)} %select_n.29, s32[]{:T(128)S(6)} %select_n.28, f32[24,4,4,128]{3,2,1,0:T(4,128)S(1)} %bitcast.100, f32[24,4]{1,0:T(8,128)S(1)} %fusion.64), kind=kOutput, calls=%fused_computation.27 | convolution fusion | flops 83423232 | bytes 6586768 | tf_op jit(solution)/shard_map/nrij,tnrj->tni/dot_general | solution.py:37
  45.2 0.0 copy-start.1
  45.2 0.0 copy-start.2
  45.2 1.5 %collective-permute-start.3 = (f32[4,256]{1,0:T(4,128)S(1)}, f32[4,256]{1,0:T(4,128)S(1)}, u32[]{:S(2)}, u32[]{:S(2)}) collective-permute-start(f32[4,256]{1,0:T(4,128)S(1)} %get-tuple-element.10), channel_id=1, source_target_pairs={{16,0},{32,16},{48,32},{64,48},{80,64},{96,80},{112,96},{128,112},... | collective-permute-start | bytes 12296 | tf_op jit(solution)/shard_map/ppermute | solution.py:20
  46.8 0.0 collective-permute-start.2
  47.5 0.6 collective-permute-done.3
  48.1 2.9 %collective-permute-done.2 = f32[4,256]{1,0:T(4,128)S(1)} collective-permute-done((f32[4,256]{1,0:T(4,128)S(1)}, f32[4,256]{1,0:T(4,128)S(1)}, u32[]{:S(2)}, u32[]{:S(2)}) %collective-permute-start.2) | collective-permute-done | bytes 4128 | tf_op jit(solution)/shard_map/ppermute | solution.py:17
  51.0 0.7 gather_fusion.1
  51.8 7.8 %fusion.10 = f32[24,4,128,1]{2,1,3,0:T(4,128)S(1)} fusion(f32[]{:T(128)} %bitcast.3, f32[]{:T(128)S(6)} %sub.16, bf16[2,24,4,128,128]{4,3,2,1,0:T(8,128)(2,1)} %param.12, s32[]{:T(128)S(6)} %select_n.29, s32[]{:T(128)S(6)} %select_n.28, f32[24,4,4,128]{3,2,1,0:T(4,128)S(1)} %bitcast.103, f32[24,4]{1,0:T(8,128)S(1)} %fusion.64), kind=kOutput, calls=%fused_computation.20 | convolution fusion | flops 83410944 | bytes 6537616 | tf_op jit(solution)/shard_map/nrij,tnrj->tni/dot_general | solution.py:37
  59.6 0.1 all_to_all.54
  59.7 0.7 copy.30
  60.3 5.7 %all-to-all-start.2 = ((f32[4,16,192]{2,0,1:T(4,128)}), f32[4,16,192]{2,0,1:T(4,128)S(1)}, u32[]{:S(2)}, u32[]{:S(2)}) async-start(f32[4,16,192]{2,0,1:T(4,128)} %copy.30), calls=%async_computation.2 | async-start | bytes 131072 | tf_op jit(solution)/shard_map/all_to_all | solution.py:70
  66.0 0.0 collective-permute-start.5
  66.0 0.5 collective-permute-start.4
  66.5 4.9 %all-to-all-done.2 = f32[4,16,192]{2,0,1:T(4,128)S(1)} async-done(((f32[4,16,192]{2,0,1:T(4,128)}), f32[4,16,192]{2,0,1:T(4,128)S(1)}, u32[]{:S(2)}, u32[]{:S(2)}) %all-to-all-start.2) | async-done | bytes 49184 | tf_op jit(solution)/shard_map/all_to_all | solution.py:70
  71.5 0.2 fusion.63
  71.7 0.6 all_to_all.58
  72.4 5.7 %all-to-all-start.3 = ((f32[16,4,192]{2,1,0:T(4,128)}), f32[16,4,192]{2,1,0:T(4,128)S(1)}, u32[]{:S(2)}, u32[]{:S(2)}) async-start(f32[16,4,192]{2,1,0:T(4,128)} %all_to_all.58), calls=%async_computation.3 | async-start | bytes 131072 | tf_op jit(solution)/shard_map/all_to_all | solution.py:72
  78.0 0.7 gather_fusion.2
  78.8 4.7 %all-to-all-done.3 = f32[16,4,192]{2,1,0:T(4,128)S(1)} async-done(((f32[16,4,192]{2,1,0:T(4,128)}), f32[16,4,192]{2,1,0:T(4,128)S(1)}, u32[]{:S(2)}, u32[]{:S(2)}) %all-to-all-start.3) | async-done | bytes 49184 | tf_op jit(solution)/shard_map/all_to_all | solution.py:72
  83.5 0.1 mul.156
  83.6 7.8 %fusion.28 = f32[4,3072]{1,0:T(4,128)S(1)} fusion(f32[4,3072]{1,0:T(4,128)S(1)} %mul.156, f32[]{:T(128)} %bitcast.26, f32[]{:T(128)S(6)} %sub.17, bf16[2,24,4,128,128]{4,3,2,1,0:T(8,128)(2,1)} %param.11, s32[]{:T(128)S(6)} %select_n.29, s32[]{:T(128)S(6)} %select_n.28, f32[24,4,4,128]{3,2,1,0:T(4,128)S(1)} %bitcast.101, f32[24,4]{1,0:T(8,128)S(1)} %fusion.64), kind=kOutput, calls=%fused_computation.28 | convolution fusion | flops 83423232 | bytes 6586768 | tf_op jit(solution)/shard_map/nrij,tnrj->tni/dot_general | solution.py:37
  91.4 0.0 collective-permute-start.7
  91.4 0.5 collective-permute-start.6
  91.9 0.8 collective-permute-done.7
  92.8 2.9 %collective-permute-done.6 = f32[4,256]{1,0:T(4,128)S(1)} collective-permute-done((f32[4,256]{1,0:T(4,128)S(1)}, f32[4,256]{1,0:T(4,128)S(1)}, u32[]{:S(2)}, u32[]{:S(2)}) %collective-permute-start.6) | collective-permute-done | bytes 4128 | tf_op jit(solution)/shard_map/ppermute | solution.py:17
  95.7 0.7 gather_fusion.3
  96.4 8.4 %fusion.16 = f32[4,3072]{1,0:T(4,128)} fusion(f32[]{:T(128)} %bitcast.26, f32[]{:T(128)S(6)} %sub.17, bf16[2,24,4,128,128]{4,3,2,1,0:T(8,128)(2,1)} %param.12, s32[]{:T(128)S(6)} %select_n.29, s32[]{:T(128)S(6)} %select_n.28, f32[24,4,4,128]{3,2,1,0:T(4,128)S(1)} %bitcast.102, f32[24,4]{1,0:T(8,128)S(1)} %fusion.64), kind=kOutput, calls=%fused_computation.24 | convolution fusion | flops 83410944 | bytes 6537616 | tf_op jit(solution)/shard_map/nrij,tnrj->tni/dot_general | solution.py:37
  (22 shorter events, 0.2 us)
Async XLA Ops:
  0.0 23.1 %copy-start = (f32[64,64]{1,0:T(8,128)S(1)}, f32[64,64]{1,0:T(8,128)}, u32[]{:S(2)}) copy-start(f32[64,64]{1,0:T(8,128)} %param.17) | copy-start | bytes 49156
  1.6 21.5 %all-to-all-start = ((f32[4,16,192]{2,0,1:T(4,128)}), f32[4,16,192]{2,0,1:T(4,128)S(1)}, u32[]{:S(2)}, u32[]{:S(2)}) async-start(f32[4,16,192]{2,0,1:T(4,128)} %copy.25), calls=%async_computation | async-start | bytes 131072 | tf_op jit(solution)/shard_map/all_to_all | solution.py:70
  9.6 22.3 %collective-permute-start.1 = (f32[4,256]{1,0:T(4,128)S(1)}, f32[4,256]{1,0:T(4,128)S(1)}, u32[]{:S(2)}, u32[]{:S(2)}) collective-permute-start(f32[4,256]{1,0:T(4,128)S(1)} %get-tuple-element.12), channel_id=1, source_target_pairs={{16,0},{32,16},{48,32},{64,48},{80,64},{96,80},{112,96},{128,112},... | collective-permute-start | bytes 12296 | tf_op jit(solution)/shard_map/ppermute | solution.py:20
  14.3 17.6 %collective-permute-start = (f32[4,256]{1,0:T(4,128)S(1)}, f32[4,256]{1,0:T(4,128)S(1)}, u32[]{:S(2)}, u32[]{:S(2)}) collective-permute-start(f32[4,256]{1,0:T(4,128)S(1)} %get-tuple-element.11), channel_id=1, source_target_pairs={{0,16},{16,32},{32,48},{48,64},{64,80},{80,96},{96,112},{112,128},... | collective-permute-start | bytes 12296 | tf_op jit(solution)/shard_map/ppermute | solution.py:17
  24.6 12.6 %all-to-all-start.1 = ((f32[16,4,192]{2,1,0:T(4,128)}), f32[16,4,192]{2,1,0:T(4,128)S(1)}, u32[]{:S(2)}, u32[]{:S(2)}) async-start(f32[16,4,192]{2,1,0:T(4,128)} %all_to_all.52), calls=%async_computation.1 | async-start | bytes 131072 | tf_op jit(solution)/shard_map/all_to_all | solution.py:72
  45.2 26.3 %copy-start.1 = (f32[64]{0:T(128)S(1)}, f32[64]{0:T(128)}, u32[]{:S(2)}) copy-start(f32[64]{0:T(128)} %param.18) | copy-start | bytes 772
  45.2 26.3 %copy-start.2 = (f32[64]{0:T(128)S(1)}, f32[64]{0:T(128)}, u32[]{:S(2)}) copy-start(f32[64]{0:T(128)} %param.19) | copy-start | bytes 772
  45.2 2.9 %collective-permute-start.3 = (f32[4,256]{1,0:T(4,128)S(1)}, f32[4,256]{1,0:T(4,128)S(1)}, u32[]{:S(2)}, u32[]{:S(2)}) collective-permute-start(f32[4,256]{1,0:T(4,128)S(1)} %get-tuple-element.10), channel_id=1, source_target_pairs={{16,0},{32,16},{48,32},{64,48},{80,64},{96,80},{112,96},{128,112},... | collective-permute-start | bytes 12296 | tf_op jit(solution)/shard_map/ppermute | solution.py:20
  46.8 4.2 %collective-permute-start.2 = (f32[4,256]{1,0:T(4,128)S(1)}, f32[4,256]{1,0:T(4,128)S(1)}, u32[]{:S(2)}, u32[]{:S(2)}) collective-permute-start(f32[4,256]{1,0:T(4,128)S(1)} %get-tuple-element.9), channel_id=1, source_target_pairs={{0,16},{16,32},{32,48},{48,64},{64,80},{80,96},{96,112},{112,128},... | collective-permute-start | bytes 12296 | tf_op jit(solution)/shard_map/ppermute | solution.py:17
  60.3 11.1 %all-to-all-start.2 = ((f32[4,16,192]{2,0,1:T(4,128)}), f32[4,16,192]{2,0,1:T(4,128)S(1)}, u32[]{:S(2)}, u32[]{:S(2)}) async-start(f32[4,16,192]{2,0,1:T(4,128)} %copy.30), calls=%async_computation.2 | async-start | bytes 131072 | tf_op jit(solution)/shard_map/all_to_all | solution.py:70
  66.0 12.0 %collective-permute-start.5 = (f32[4,256]{1,0:T(4,128)S(1)}, f32[4,256]{1,0:T(4,128)S(1)}, u32[]{:S(2)}, u32[]{:S(2)}) collective-permute-start(f32[4,256]{1,0:T(4,128)S(1)} %get-tuple-element.8), channel_id=1, source_target_pairs={{16,0},{32,16},{48,32},{64,48},{80,64},{96,80},{112,96},{128,112},... | collective-permute-start | bytes 12296 | tf_op jit(solution)/shard_map/ppermute | solution.py:20
  66.0 12.0 %collective-permute-start.4 = (f32[4,256]{1,0:T(4,128)S(1)}, f32[4,256]{1,0:T(4,128)S(1)}, u32[]{:S(2)}, u32[]{:S(2)}) collective-permute-start(f32[4,256]{1,0:T(4,128)S(1)} %get-tuple-element.7), channel_id=1, source_target_pairs={{0,16},{16,32},{32,48},{48,64},{64,80},{80,96},{96,112},{112,128},... | collective-permute-start | bytes 12296 | tf_op jit(solution)/shard_map/ppermute | solution.py:17
  72.4 11.1 %all-to-all-start.3 = ((f32[16,4,192]{2,1,0:T(4,128)}), f32[16,4,192]{2,1,0:T(4,128)S(1)}, u32[]{:S(2)}, u32[]{:S(2)}) async-start(f32[16,4,192]{2,1,0:T(4,128)} %all_to_all.58), calls=%async_computation.3 | async-start | bytes 131072 | tf_op jit(solution)/shard_map/all_to_all | solution.py:72
  91.4 1.3 %collective-permute-start.7 = (f32[4,256]{1,0:T(4,128)S(1)}, f32[4,256]{1,0:T(4,128)S(1)}, u32[]{:S(2)}, u32[]{:S(2)}) collective-permute-start(f32[4,256]{1,0:T(4,128)S(1)} %get-tuple-element.6), channel_id=1, source_target_pairs={{16,0},{32,16},{48,32},{64,48},{80,64},{96,80},{112,96},{128,112},... | collective-permute-start | bytes 12296 | tf_op jit(solution)/shard_map/ppermute | solution.py:20
  91.4 4.3 %collective-permute-start.6 = (f32[4,256]{1,0:T(4,128)S(1)}, f32[4,256]{1,0:T(4,128)S(1)}, u32[]{:S(2)}, u32[]{:S(2)}) collective-permute-start(f32[4,256]{1,0:T(4,128)S(1)} %get-tuple-element.5), channel_id=1, source_target_pairs={{0,16},{16,32},{32,48},{48,64},{64,80},{80,96},{96,112},{112,128},... | collective-permute-start | bytes 12296 | tf_op jit(solution)/shard_map/ppermute | solution.py:17
where the time goes:
time: 107 us; the launch traced here: 105 us
  starting transfers between devices  33.1 us (31%)
  matrix products  32.9 us (31%)
  waiting for transfers between devices  20.8 us (19%)
  local copies, waits for them, and re-layouts  10.4 us (10%)
  between operations  5.32 us (5%)
  other arithmetic  2.32 us (2%)
    dot_general x4, matrix products, apply_local(): jnp.einsum('nrij,tnrj->tni', matrix, picked, precision=lax.Precision.HIGH...  31.8 us
    all_to_all x2, starting transfers between devices, per_device(): lax.all_to_all(field, 'trc', split_axis=1, concat_axis=0, tiled=True)  13 us
    all_to_all x2, starting transfers between devices, per_device(): lax.all_to_all(terms, 'trc', split_axis=0, concat_axis=1, tiled=True)  12.9 us
    all_to_all x2, waiting for transfers between devices, per_device(): lax.all_to_all(terms, 'trc', split_axis=0, concat_axis=1, tiled=True)  8.55 us
    ppermute x4, starting transfers between devices, extended(): lax.ppermute(lax.slice_in_dim(block, 0, width, axis=dim), axis, backward)  6.31 us
    ppermute x4, waiting for transfers between devices, extended(): lax.ppermute(lax.slice_in_dim(block, block.shape[dim] - width, None, axis...  5.85 us
    all_to_all x2, waiting for transfers between devices, per_device(): lax.all_to_all(field, 'trc', split_axis=1, concat_axis=0, tiled=True)  4.92 us
    gather x4, local copies, waits for them, and re-layouts, apply_local(): picked = split[:, column_blocks] * used[None, :, :, None]  2.83 us
  transfers between devices with their start and end apart: 12, of which 7 were waited for; matrix products, arithmetic and copies ran while one was open for 8% of the time, Pallas kernels for 0%

commit v1 on v0

v1 whole, which is shorter than its diff:
```python
import jax
import jax.numpy as jnp
from jax import lax
from jax.experimental import pallas as pl
from jax.experimental.pallas import tpu as pltpu
from jax.sharding import PartitionSpec as P

REACH = 2
DAYS = 30
STEPS = 2
LOW = 2 * REACH
HIGH = 2 * (REACH - 1)
F32 = jnp.float32
BF16 = jnp.bfloat16
MIB = 1 << 20
NT = (((1,), (1,)), ((), ()))


def split_store(ref, where, value):
    half = value.shape[0]
    high = value.astype(BF16)
    ref[where, 0:half, :] = high
    ref[where, half : 2 * half, :] = (value - high.astype(F32)).astype(BF16)


def combine(product, coef_ref, step):
    block = product.shape[1] // 2
    half = product.shape[0] // 2
    mixed = coef_ref[step, 0] * product[:, :block] + coef_ref[step, 1] * product[:, block:]
    return mixed[:half] + mixed[half:]


def own_row(values_ref, blocks_ref, cols_ref, row, shift, coef_ref, step):
    width = blocks_ref.shape[2]
    left = jnp.concatenate([values_ref[cols_ref[row, r] - shift] for r in range(width)], axis=1)
    right = jnp.concatenate(
        [
            jnp.concatenate([blocks_ref[m, row, r] for r in range(width)], axis=1)
            for m in range(2)
        ],
        axis=0,
    )
    product = lax.dot_general(left, right, NT, preferred_element_type=F32)
    return combine(product, coef_ref, step)


def edge_row(values_ref, edge_ref, row, first, coef_ref, step):
    width = edge_ref.shape[2]
    left = jnp.concatenate([values_ref[first + d] for d in range(width)], axis=1)
    right = jnp.concatenate(
        [
            jnp.concatenate([edge_ref[m, row, d].astype(BF16) for d in range(width)], axis=1)
            for m in range(2)
        ],
        axis=0,
    )
    product = lax.dot_general(left, right, NT, preferred_element_type=F32)
    return combine(product, coef_ref, step)


def mixing_tile(mix_ref):
    mix = mix_ref[...]
    high = mix.astype(BF16)
    low = (mix - high.astype(F32)).astype(BF16)
    return jnp.concatenate([high, low], axis=0)


def half_source(values, mixing, bias_ref, rate_ref):
    both = lax.dot_general(
        mixing, values, (((1,), (0,)), ((), ())), preferred_element_type=F32
    )
    half = both.shape[0] // 2
    inner = both[:half] + both[half:] + bias_ref[...]
    return rate_ref[...] * inner * jnp.exp(-0.125 * inner * inner)


def edges_kernel(position_ref, cols_ref, low_ref, high_ref, to_right_ref, to_left_ref):
    reach_cols = low_ref.shape[2]
    for source_ref, target_ref, start in (
        (low_ref, to_right_ref, position_ref[0]),
        (high_ref, to_left_ref, 0),
    ):
        for row in range(source_ref.shape[1]):
            n = start + row
            for d in range(reach_cols):
                wanted = n + LOW - REACH + d
                slot = jnp.int32(0)
                scale = jnp.float32(0.0)
                for r in range(reach_cols):
                    hit = cols_ref[n, r] == wanted
                    slot = jnp.where(hit, r, slot)
                    scale = jnp.where(hit, 1.0, scale)
                for m in range(2):
                    target_ref[m, row, d] = source_ref[m, row, slot].astype(F32) * scale


def pack_edges(explicit_blocks, cols):
    months, rows, width, block, _ = explicit_blocks.shape
    spec = lambda count, at: pl.BlockSpec(
        (months, count, width, block, block), lambda i: (0, at, 0, 0, 0)
    )
    smem = pl.BlockSpec(memory_space=pltpu.SMEM)
    shape = lambda count: jax.ShapeDtypeStruct((months, count, width, block, block), F32)
    return pl.pallas_call(
        edges_kernel,
        grid=(1,),
        in_specs=[
            smem,
            smem,
            spec(REACH, rows // REACH - 1),
            spec(REACH - 1, 0),
        ],
        out_specs=[spec(REACH, 0), spec(REACH - 1, 0)],
        out_shape=[shape(REACH), shape(REACH - 1)],
        name="edges",
    )(jnp.full((1,), rows - REACH, jnp.int32), cols, explicit_blocks, explicit_blocks)


def first_kernel(
    cols_ref, coef_ref, field_ref, explicit_ref, implicit_ref, left_ref, right_ref,
    mix_ref, bias_ref, rate_ref, low_ref, high_ref, field_out_ref, values_ref, middle_ref,
):
    rows = explicit_ref.shape[1]
    block = explicit_ref.shape[-1]
    tracers = mix_ref.shape[0]
    ext = rows + LOW + HIGH
    zero = jnp.zeros((2 * tracers, block), BF16)
    values_ref[ext] = zero
    middle_ref[ext - REACH] = zero
    for b in range(ext):
        split_store(values_ref, b, field_ref[pl.ds(b, tracers, stride=ext), :])
    mixing = mixing_tile(mix_ref)

    def finish(frame, product):
        source = half_source(values_ref[frame + REACH], mixing, bias_ref, rate_ref)
        split_store(middle_ref, frame, product + source)

    for row in range(REACH):
        finish(row, edge_row(values_ref, left_ref, row, row, coef_ref, 0))
    for row in range(REACH - 1):
        frame = rows + REACH + row
        finish(frame, edge_row(values_ref, right_ref, row, frame, coef_ref, 0))

    def explicit_row(row, carry):
        finish(row + REACH, own_row(values_ref, explicit_ref, cols_ref, row, 0, coef_ref, 0))
        return carry

    lax.fori_loop(0, rows, explicit_row, 0, unroll=4)

    for row in range(LOW):
        result = own_row(
            middle_ref, implicit_ref, cols_ref, rows - LOW + row, REACH, coef_ref, 0
        )
        low_ref[:, row * block : (row + 1) * block] = result
        split_store(field_out_ref, rows - LOW + row, result)
    for row in range(HIGH):
        result = own_row(middle_ref, implicit_ref, cols_ref, row, REACH, coef_ref, 0)
        high_ref[:, row * block : (row + 1) * block] = result
        split_store(field_out_ref, row, result)

    def implicit_row(row, carry):
        split_store(
            field_out_ref,
            row,
            own_row(middle_ref, implicit_ref, cols_ref, row, REACH, coef_ref, 0),
        )
        return carry

    lax.fori_loop(HIGH, rows - LOW, implicit_row, 0, unroll=3)


def inner_kernel(
    cols_ref, coef_ref, field_ref, explicit_ref, mix_ref, bias_ref, rate_ref,
    middle_ref, values_ref,
):
    rows = explicit_ref.shape[1]
    values_ref[LOW : LOW + rows] = field_ref[...]
    values_ref[rows + LOW + HIGH] = jnp.zeros(values_ref.shape[1:], BF16)
    mixing = mixing_tile(mix_ref)

    def explicit_row(row, carry):
        product = own_row(values_ref, explicit_ref, cols_ref, row, 0, coef_ref, 1)
        source = half_source(values_ref[row + LOW], mixing, bias_ref, rate_ref)
        split_store(middle_ref, row, product + source)
        return carry

    lax.fori_loop(REACH, rows - REACH + 1, explicit_row, 0, unroll=3)


def last_kernel(
    cols_ref, coef_ref, place_ref, low_in_ref, high_in_ref, field_ref, middle_in_ref,
    explicit_ref, implicit_ref, left_ref, right_ref, mix_ref, bias_ref, rate_ref,
    out_ref, values_ref, middle_ref, result_ref,
):
    rows = explicit_ref.shape[1]
    block = explicit_ref.shape[-1]
    tracers = mix_ref.shape[0]
    ext = rows + LOW + HIGH
    zero = jnp.zeros((2 * tracers, block), BF16)
    values_ref[ext] = zero
    middle_ref[ext - REACH] = zero
    values_ref[LOW : LOW + rows] = field_ref[...]
    middle_ref[2 * REACH : rows + 1] = middle_in_ref[REACH : rows - REACH + 1]
    for b in range(LOW):
        split_store(values_ref, b, low_in_ref[:, b * block : (b + 1) * block])
    for b in range(HIGH):
        split_store(values_ref, LOW + rows + b, high_in_ref[:, b * block : (b + 1) * block])
    mixing = mixing_tile(mix_ref)

    def finish(frame, product):
        source = half_source(values_ref[frame + REACH], mixing, bias_ref, rate_ref)
        split_store(middle_ref, frame, product + source)

    for row in range(REACH):
        finish(row, edge_row(values_ref, left_ref, row, row, coef_ref, 1))
    for row in range(REACH - 1):
        frame = rows + REACH + row
        finish(frame, edge_row(values_ref, right_ref, row, frame, coef_ref, 1))
    for row in [*range(REACH), *range(rows - REACH + 1, rows)]:
        finish(row + REACH, own_row(values_ref, explicit_ref, cols_ref, row, 0, coef_ref, 1))

    for row in range(rows):
        result_ref[:, row * block : (row + 1) * block] = own_row(
            middle_ref, implicit_ref, cols_ref, row, REACH, coef_ref, 1
        )
    mine = out_ref.shape[0]
    place = place_ref[0]
    pair = result_ref[pl.ds(pl.multiple_of((place // 2) * 2 * mine, 2 * mine), 2 * mine), :]
    out_ref[...] = jnp.where(place % 2 == 0, pair[:mine], pair[mine:])


def call(kernel, name, smem_count, args, outs, scratch, flops, limit):
    smem = pl.BlockSpec(memory_space=pltpu.SMEM)
    vmem = pl.BlockSpec(memory_space=pltpu.VMEM)
    return pl.pallas_call(
        kernel,
        in_specs=[smem] * smem_count + [vmem] * (len(args) - smem_count),
        out_specs=[vmem] * len(outs),
        out_shape=outs,
        scratch_shapes=scratch,
        compiler_params=pltpu.CompilerParams(vmem_limit_bytes=limit * MIB),
        cost_estimate=pl.CostEstimate(flops=flops, bytes_accessed=8 * MIB, transcendentals=0),
        name=name,
    )(*args)


def per_device(
    tracers,
    explicit_blocks,
    implicit_blocks,
    column_blocks,
    block_count,
    month_pair,
    weight_num,
    source_mix,
    source_bias,
    source_rate,
):
    rows, width = column_blocks.shape
    block = explicit_blocks.shape[-1]
    parts = lax.axis_size("pts")
    groups = lax.axis_size("trc")
    mine = tracers.shape[0]
    total = source_mix.shape[0]
    ext = rows + LOW + HIGH
    forward = [(i, (i + 1) % parts) for i in range(parts)]
    backward = [(target, source) for source, target in forward]

    used = jnp.arange(width)[None, :] < block_count[:, None]
    cols = (column_blocks - lax.axis_index("pts") * rows + LOW) % (rows * parts)
    cols = jnp.where(used, cols, ext).astype(jnp.int32)
    weight = weight_num.astype(F32) / DAYS
    straight = month_pair[0] == 0
    coef = jnp.stack(
        [jnp.where(straight, 1.0 - weight, weight), jnp.where(straight, weight, 1.0 - weight)],
        axis=1,
    )
    mix = jnp.concatenate([source_mix, source_mix], axis=1)
    bias = source_bias[:, None]
    rate = 0.5 * source_rate[:, None]
    place = lax.axis_index("trc").astype(jnp.int32).reshape(1)

    low = lax.ppermute(tracers[:, -LOW * block :], "pts", forward)
    high = lax.ppermute(tracers[:, : HIGH * block], "pts", backward)
    to_right, to_left = pack_edges(explicit_blocks, cols)
    extended = jnp.concatenate([low, tracers, high], axis=1)
    extended = extended.reshape(mine * ext, block)
    gathered = lax.all_to_all(
        jnp.broadcast_to(extended[None], (groups,) + extended.shape),
        "trc", split_axis=0, concat_axis=0, tiled=True,
    )
    gathered = gathered.reshape(total * ext, block)
    left = lax.ppermute(to_right, "pts", forward)
    right = lax.ppermute(to_left, "pts", backward)

    shape = jax.ShapeDtypeStruct
    stack = lambda count: pltpu.VMEM((count, 2 * total, block), BF16)
    one = 2 * 2 * total * 2 * block * width * block
    low, high, field = call(
        first_kernel, "first", 2,
        (cols, coef, gathered, explicit_blocks, implicit_blocks, left, right, mix, bias, rate),
        [
            shape((total, LOW * block), F32),
            shape((total, HIGH * block), F32),
            shape((rows, 2 * total, block), BF16),
        ],
        [stack(ext + 1), stack(ext - REACH + 1)],
        51 * one, 26,
    )
    low = lax.ppermute(low, "pts", forward)
    high = lax.ppermute(high, "pts", backward)
    (middle,) = call(
        inner_kernel, "inner", 2,
        (cols, coef, field, explicit_blocks, mix, bias, rate),
        [shape((rows, 2 * total, block), BF16)],
        [stack(ext + 1)],
        21 * one, 18,
    )
    (advanced,) = call(
        last_kernel, "last", 3,
        (
            cols, coef, place, low, high, field, middle, explicit_blocks, implicit_blocks,
            left, right, mix, bias, rate,
        ),
        [shape((mine, rows * block), F32)],
        [stack(ext + 1), stack(ext - REACH + 1), pltpu.VMEM((total, rows * block), F32)],
        30 * one, 26,
    )
    return advanced


def solution(mesh):
    in_specs = (
        P("trc", "pts"),
        P(None, "pts", None, None, None),
        P(None, "pts", None, None, None),
        P("pts", None),
        P("pts"),
        P(),
        P(),
        P(),
        P(),
        P(),
    )
    out_specs = P("trc", "pts")
    return jax.shard_map(
        per_device, mesh=mesh, in_specs=in_specs, out_specs=out_specs, check_vma=False
    )
```

time: 107 us -> 64.5 us (0.60)
  the two profiles are of different devices: /device:TPU:16 before, /device:TPU:65 now
where the time goes in v1:
time: 64.5 us; the launch traced here: 64 us
  Pallas kernels  18 us (28%)
  waiting for transfers between devices  15.5 us (24%)
  local copies, waits for them, and re-layouts  14.1 us (22%)
  starting transfers between devices  14 us (22%)
  other arithmetic  2.19 us (3%)
    pallas_call x3, Pallas kernels, call(): pl.pallas_call(kernel, in_specs=[smem] * smem_count + [vmem] * (len(args)...  15.6 us
    unnamed x24, local copies, waits for them, and re-layouts  11.2 us
    ppermute x1, waiting for transfers between devices, per_device(): right = lax.ppermute(to_left, 'pts', backward)  9.49 us
    all_to_all x1, starting transfers between devices, per_device(): lax.all_to_all(jnp.broadcast_to(extended[None], (groups,) + extended.shap...  6.75 us
    all_to_all x1, waiting for transfers between devices, per_device(): lax.all_to_all(jnp.broadcast_to(extended[None], (groups,) + extended.shap...  6.03 us
    ppermute x1, starting transfers between devices, per_device(): low = lax.ppermute(low, 'pts', forward)  4.26 us
    pallas_call x1, Pallas kernels, pack_edges(): pl.pallas_call(edges_kernel, grid=(1,), in_specs=[smem, smem, spec(REACH,...  2.44 us
    ppermute x1, starting transfers between devices, per_device(): low = lax.ppermute(tracers[:, -LOW * block:], 'pts', forward)  1.53 us
  transfers between devices with their start and end apart: 7, of which 2 were waited for; matrix products, arithmetic and copies ran while one was open for 7% of the time, Pallas kernels for 10%

profile of v1, /device:TPU:65, one launch (start us, length us, event | category | flops | bytes accessed | tf_op | source)
XLA Modules:
  0.0 64.0 jit_solution(1778042195580589451)
XLA Ops:
  0.0 0.7 %slice.11 = f32[4,256]{1,0:T(4,128)S(1)} slice(f32[4,3072]{1,0:T(4,128)} %param.10), slice={[0:4], [0:256]} | slice | bytes 8192 | tf_op jit(solution)/shard_map/slice | solution.py:284
  0.7 0.7 %collective-permute-start.1 = (f32[4,256]{1,0:T(4,128)S(1)}, f32[4,256]{1,0:T(4,128)S(1)}, u32[]{:S(2)}, u32[]{:S(2)}) collective-permute-start(f32[4,256]{1,0:T(4,128)S(1)} %slice.11), channel_id=1, source_target_pairs={{16,0},{32,16},{48,32},{64,48},{80,64},{96,80},{112,96},{128,112},... | collective-permute-start | bytes 12296 | tf_op jit(solution)/shard_map/ppermute | solution.py:284
  1.4 0.7 %slice.10 = f32[4,512]{1,0:T(4,128)S(1)} slice(f32[4,3072]{1,0:T(4,128)} %param.10), slice={[0:4], [2560:3072]} | slice | bytes 16384 | tf_op jit(solution)/shard_map/slice | solution.py:283
  2.1 1.5 %collective-permute-start = (f32[4,512]{1,0:T(4,128)S(1)}, f32[4,512]{1,0:T(4,128)S(1)}, u32[]{:S(2)}, u32[]{:S(2)}) collective-permute-start(f32[4,512]{1,0:T(4,128)S(1)} %slice.10), channel_id=1, source_target_pairs={{0,16},{16,32},{32,48},{48,64},{64,80},{80,96},{96,112},{112,128},... | collective-permute-start | bytes 24584 | tf_op jit(solution)/shard_map/ppermute | solution.py:283
  3.6 0.7 %subtract_add_fusion = s32[24,4]{0,1:T(4,128)S(1)} fusion(s32[24,4]{0,1:T(4,128)} %param.13, s32[]{:T(128)S(6)} %mul.11), kind=kLoop, calls=%fused_computation.5 | loop fusion | flops 192 | bytes 772 | tf_op jit(solution)/shard_map/add | solution.py:270
  4.3 0.1 copy.22
  4.4 1.3 %fusion.cols_ref = s32[24,4]{1,0:T(8,128)} fusion(s32[24,4]{1,0:T(8,128)S(1)} %copy.22, s32[24]{0:T(128)} %param.14), kind=kLoop, calls=%fused_computation.3 | loop fusion | flops 768 | bytes 864 | tf_op jit(solution)/shard_map/jit(_where)/select_n | solution.py:271
  5.7 0.0 copy-start.6
  5.7 0.0 copy-start.9
  5.7 0.0 copy-start.11
  5.7 0.0 copy-start.7
  5.7 0.0 copy-start.5
  5.7 2.4 %edges.1 = (f32[2,2,4,128,128]{4,3,2,1,0:T(8,128)}, f32[2,1,4,128,128]{4,3,2,1,0:T(8,128)}) custom-call(s32[1]{0:T(128)} %constant.35.clone.1.position_ref, s32[24,4]{1,0:T(8,128)} %fusion.cols_ref, bf16[2,24,4,128,128]{4,3,2,1,0:T(8,128)(2,1)} %explicit_ref.5, bf16[2,24,4,128,128]{4,3,2,1,0:T(8,128)(2,1)} %explicit_ref.5), custom_call_target="tpu_custom_call" | custom-call | tf_op jit(solution)/shard_map/edges/pallas_call | solution.py:104
  8.2 0.5 collective-permute-start.2
  8.7 0.0 collective-permute-done.1
  8.7 0.0 collective-permute-done
  8.7 0.0 copy-done.6
  8.8 1.0 %broadcast_in_dim.19 = f32[16,120,128]{2,1,0:T(8,128)} broadcast(f32[120,128]{1,0:T(8,128)S(1)} %broadcast_in_dim.18), dimensions={1,2} | broadcast | bytes 1044480 | tf_op jit(solution)/shard_map/broadcast_in_dim | solution.py:289
  9.8 6.8 %all-to-all-start = ((f32[16,120,128]{2,1,0:T(8,128)}), f32[16,120,128]{2,1,0:T(8,128)S(1)}, u32[]{:S(2)}, u32[]{:S(2)}) async-start(f32[16,120,128]{2,1,0:T(8,128)} %broadcast_in_dim.19), calls=%async_computation | async-start | bytes 1966080 | tf_op jit(solution)/shard_map/all_to_all | solution.py:288
  16.5 0.3 collective-permute-start.3
  16.8 0.0 copy-done.10
  16.9 0.0 copy-done.9
  16.9 0.1 copy.24
  17.0 0.1 copy.23
  17.1 0.0 copy-done.8
  17.1 0.1 copy.25.bias_ref
  17.2 0.0 copy-done.11
  17.2 0.1 copy.26.rate_ref
  17.3 0.1 pad_maximum_fusion.2.coef_ref
  17.4 0.0 copy-done.7
  17.4 0.1 pad_maximum_fusion.1.mix_ref
  17.4 9.5 %collective-permute-done.3.right_ref = f32[2,1,4,128,128]{4,3,2,1,0:T(8,128)S(1)} collective-permute-done((f32[2,1,4,128,128]{4,3,2,1,0:T(8,128)}, f32[2,1,4,128,128]{4,3,2,1,0:T(8,128)S(1)}, u32[]{:S(2)}, u32[]{:S(2)}) %collective-permute-start.3) | collective-permute-done | bytes 524320 | tf_op jit(solution)/shard_map/ppermute | solution.py:294
  26.9 6.0 %all-to-all-done = f32[16,120,128]{2,1,0:T(8,128)S(1)} async-done(((f32[16,120,128]{2,1,0:T(8,128)}), f32[16,120,128]{2,1,0:T(8,128)S(1)}, u32[]{:S(2)}, u32[]{:S(2)}) %all-to-all-start) | async-done | bytes 983072 | tf_op jit(solution)/shard_map/all_to_all | solution.py:288
  33.0 0.0 collective-permute-done.2.left_ref
  33.0 0.0 copy-done.5
  33.0 2.8 %copy-done = bf16[2,24,4,128,128]{4,3,2,1,0:T(8,128)(2,1)S(1)} copy-done((bf16[2,24,4,128,128]{4,3,2,1,0:T(8,128)(2,1)S(1)}, bf16[2,24,4,128,128]{4,3,2,1,0:T(8,128)(2,1)}, u32[]{:S(2)}) %copy-start) | copy-done | bytes 6291480
  35.8 2.8 %copy-done.3 = bf16[2,24,4,128,128]{4,3,2,1,0:T(8,128)(2,1)S(1)} copy-done((bf16[2,24,4,128,128]{4,3,2,1,0:T(8,128)(2,1)S(1)}, bf16[2,24,4,128,128]{4,3,2,1,0:T(8,128)(2,1)}, u32[]{:S(2)}) %copy-start.3) | copy-done | bytes 6291480
  38.5 7.7 %first.1 = (f32[64,512]{1,0:T(8,128)}, f32[64,256]{1,0:T(8,128)S(1)}, bf16[24,128,128]{2,1,0:T(8,128)(2,1)S(1)}) custom-call(s32[24,4]{1,0:T(8,128)S(1)} %copy-done.5, f32[2,2]{1,0:T(2,128)S(1)} %pad_maximum_fusion.2.coef_ref, f32[1920,128]{1,0:T(8,128)S(1)} %bitcast.11, bf16[2,24,4,128,128]{4,3,2,1,0:T(8,128)(2,1)S(1)} %copy-done, ...), custom_call_target="tpu_custom_call" | custom-call | flops 1711276032 | bytes 8388608 | tf_op jit(solution)/shard_map/first/pallas_call | solution.py:235
  46.3 4.3 %collective-permute-start.4 = (f32[64,512]{1,0:T(8,128)}, f32[64,512]{1,0:T(8,128)S(1)}, u32[]{:S(2)}, u32[]{:S(2)}) collective-permute-start(f32[64,512]{1,0:T(8,128)} %get-tuple-element.12), channel_id=1, source_target_pairs={{0,16},{16,32},{32,48},{48,64},{64,80},{80,96},{96,112},{112,128},... | collective-permute-start | bytes 393224 | tf_op jit(solution)/shard_map/ppermute | solution.py:310
  50.5 0.0 collective-permute-start.5
  50.5 2.8 %copy-done.1 = bf16[2,24,4,128,128]{4,3,2,1,0:T(8,128)(2,1)S(1)} copy-done((bf16[2,24,4,128,128]{4,3,2,1,0:T(8,128)(2,1)S(1)}, bf16[2,24,4,128,128]{4,3,2,1,0:T(8,128)(2,1)}, u32[]{:S(2)}) %copy-start.1) | copy-done | bytes 6291480
  53.3 3.7 %inner.1.middle_in_ref = bf16[24,128,128]{2,1,0:T(8,128)(2,1)S(1)} custom-call(s32[24,4]{1,0:T(8,128)S(1)} %copy-done.5, f32[2,2]{1,0:T(2,128)S(1)} %pad_maximum_fusion.2.coef_ref, bf16[24,128,128]{2,1,0:T(8,128)(2,1)S(1)} %get-tuple-element.14.field_ref, bf16[2,24,4,128,128]{4,3,2,1,0:T(8,128)(2,1)S(1)} %copy-done.1, ...), custom_call_target="tpu_custom_call" | custom-call | flops 704643072 | bytes 8388608 | tf_op jit(solution)/shard_map/inner/pallas_call | solution.py:235
  57.1 0.0 collective-permute-done.5.high_in_ref
  57.1 0.0 collective-permute-done.4.low_in_ref
  57.1 0.0 copy-done.2
  57.1 0.0 copy-start.4
  57.1 2.8 %copy-done.4 = bf16[2,24,4,128,128]{4,3,2,1,0:T(8,128)(2,1)S(1)} copy-done((bf16[2,24,4,128,128]{4,3,2,1,0:T(8,128)(2,1)S(1)}, bf16[2,24,4,128,128]{4,3,2,1,0:T(8,128)(2,1)}, u32[]{:S(2)}) %copy-start.4) | copy-done | bytes 6291480
  59.9 4.2 %last.1 = f32[4,3072]{1,0:T(4,128)} custom-call(s32[24,4]{1,0:T(8,128)S(1)} %copy-done.5, f32[2,2]{1,0:T(2,128)S(1)} %pad_maximum_fusion.2.coef_ref, s32[1]{0:T(128)} %bitcast.3.place_ref, f32[64,512]{1,0:T(8,128)S(1)} %collective-permute-done.4.low_in_ref, f32[64,256]{1,0:T(8,128)S(1)} %collective-permute-done.5.high_in_ref, ...), custom_call_target="tpu_custom_call" | custom-call | flops 1006632960 | bytes 8388608 | tf_op jit(solution)/shard_map/last/pallas_call | solution.py:235
  (10 shorter events, 0.1 us)
Async XLA Ops:
  0.7 8.0 %collective-permute-start.1 = (f32[4,256]{1,0:T(4,128)S(1)}, f32[4,256]{1,0:T(4,128)S(1)}, u32[]{:S(2)}, u32[]{:S(2)}) collective-permute-start(f32[4,256]{1,0:T(4,128)S(1)} %slice.11), channel_id=1, source_target_pairs={{16,0},{32,16},{48,32},{64,48},{80,64},{96,80},{112,96},{128,112},... | collective-permute-start | bytes 12296 | tf_op jit(solution)/shard_map/ppermute | solution.py:284
  2.1 6.6 %collective-permute-start = (f32[4,512]{1,0:T(4,128)S(1)}, f32[4,512]{1,0:T(4,128)S(1)}, u32[]{:S(2)}, u32[]{:S(2)}) collective-permute-start(f32[4,512]{1,0:T(4,128)S(1)} %slice.10), channel_id=1, source_target_pairs={{0,16},{16,32},{32,48},{48,64},{64,80},{80,96},{96,112},{112,128},... | collective-permute-start | bytes 24584 | tf_op jit(solution)/shard_map/ppermute | solution.py:283
  5.7 3.0 %copy-start.6 = (f32[4,3072]{1,0:T(4,128)S(1)}, f32[4,3072]{1,0:T(4,128)}, u32[]{:S(2)}) copy-start(f32[4,3072]{1,0:T(4,128)} %param.10) | copy-start | bytes 147460
  5.7 11.1 %copy-start.10 = (s32[2]{0:T(128)S(1)}, s32[2]{0:T(128)}, u32[]{:S(2)}) copy-start(s32[2]{0:T(128)} %param.15) | copy-start | bytes 28
  5.7 11.2 %copy-start.9 = (s32[2]{0:T(128)S(1)}, s32[2]{0:T(128)}, u32[]{:S(2)}) copy-start(s32[2]{0:T(128)} %param.16) | copy-start | bytes 28
  5.7 11.4 %copy-start.8 = (f32[64]{0:T(128)S(1)}, f32[64]{0:T(128)}, u32[]{:S(2)}) copy-start(f32[64]{0:T(128)} %param.18) | copy-start | bytes 772
  5.7 11.5 %copy-start.11 = (f32[64]{0:T(128)S(1)}, f32[64]{0:T(128)}, u32[]{:S(2)}) copy-start(f32[64]{0:T(128)} %param.19) | copy-start | bytes 772
  5.7 11.7 %copy-start.7 = (f32[64,64]{1,0:T(8,128)S(1)}, f32[64,64]{1,0:T(8,128)}, u32[]{:S(2)}) copy-start(f32[64,64]{1,0:T(8,128)} %param.17) | copy-start | bytes 49156
  5.7 27.2 %copy-start.5 = (s32[24,4]{1,0:T(8,128)S(1)}, s32[24,4]{1,0:T(8,128)}, u32[]{:S(2)}) copy-start(s32[24,4]{1,0:T(8,128)} %fusion.cols_ref) | copy-start | bytes 1156
  8.2 24.8 %collective-permute-start.2 = (f32[2,2,4,128,128]{4,3,2,1,0:T(8,128)}, f32[2,2,4,128,128]{4,3,2,1,0:T(8,128)S(1)}, u32[]{:S(2)}, u32[]{:S(2)}) collective-permute-start(f32[2,2,4,128,128]{4,3,2,1,0:T(8,128)} %get-tuple-element.10), channel_id=1, source_target_pairs={{0,16},{16,32},{32,48},{48,64},{64,80},{80,96},{96,112},{112,128},... | collective-permute-start | bytes 3145736 | tf_op jit(solution)/shard_map/ppermute | solution.py:293
  9.8 23.2 %all-to-all-start = ((f32[16,120,128]{2,1,0:T(8,128)}), f32[16,120,128]{2,1,0:T(8,128)S(1)}, u32[]{:S(2)}, u32[]{:S(2)}) async-start(f32[16,120,128]{2,1,0:T(8,128)} %broadcast_in_dim.19), calls=%async_computation | async-start | bytes 1966080 | tf_op jit(solution)/shard_map/all_to_all | solution.py:288
  16.5 10.4 %collective-permute-start.3 = (f32[2,1,4,128,128]{4,3,2,1,0:T(8,128)}, f32[2,1,4,128,128]{4,3,2,1,0:T(8,128)S(1)}, u32[]{:S(2)}, u32[]{:S(2)}) collective-permute-start(f32[2,1,4,128,128]{4,3,2,1,0:T(8,128)} %get-tuple-element.11), channel_id=1, source_target_pairs={{16,0},{32,16},{48,32},{64,48},{80,64},{96,80},{112,96},{128,112},... | collective-permute-start | bytes 1572872 | tf_op jit(solution)/shard_map/ppermute | solution.py:294
  33.0 2.8 %copy-start = (bf16[2,24,4,128,128]{4,3,2,1,0:T(8,128)(2,1)S(1)}, bf16[2,24,4,128,128]{4,3,2,1,0:T(8,128)(2,1)}, u32[]{:S(2)}) copy-start(bf16[2,24,4,128,128]{4,3,2,1,0:T(8,128)(2,1)} %explicit_ref.5) | copy-start | bytes 18874372
  35.8 2.8 %copy-start.3 = (bf16[2,24,4,128,128]{4,3,2,1,0:T(8,128)(2,1)S(1)}, bf16[2,24,4,128,128]{4,3,2,1,0:T(8,128)(2,1)}, u32[]{:S(2)}) copy-start(bf16[2,24,4,128,128]{4,3,2,1,0:T(8,128)(2,1)} %implicit_ref.3) | copy-start | bytes 18874372
  46.3 10.8 %collective-permute-start.4 = (f32[64,512]{1,0:T(8,128)}, f32[64,512]{1,0:T(8,128)S(1)}, u32[]{:S(2)}, u32[]{:S(2)}) collective-permute-start(f32[64,512]{1,0:T(8,128)} %get-tuple-element.12), channel_id=1, source_target_pairs={{0,16},{16,32},{32,48},{48,64},{64,80},{80,96},{96,112},{112,128},... | collective-permute-start | bytes 393224 | tf_op jit(solution)/shard_map/ppermute | solution.py:310
  50.5 6.5 %collective-permute-start.5 = (f32[64,256]{1,0:T(8,128)S(1)}, f32[64,256]{1,0:T(8,128)S(1)}, u32[]{:S(2)}, u32[]{:S(2)}) collective-permute-start(f32[64,256]{1,0:T(8,128)S(1)} %get-tuple-element.13), channel_id=1, source_target_pairs={{16,0},{32,16},{48,32},{64,48},{80,64},{96,80},{112,96},{128,112},... | collective-permute-start | bytes 196616 | tf_op jit(solution)/shard_map/ppermute | solution.py:311
  50.5 2.8 %copy-start.1 = (bf16[2,24,4,128,128]{4,3,2,1,0:T(8,128)(2,1)S(1)}, bf16[2,24,4,128,128]{4,3,2,1,0:T(8,128)(2,1)}, u32[]{:S(2)}) copy-start(bf16[2,24,4,128,128]{4,3,2,1,0:T(8,128)(2,1)} %explicit_ref.5) | copy-start | bytes 18874372
  53.3 3.8 %copy-start.2 = (bf16[2,24,4,128,128]{4,3,2,1,0:T(8,128)(2,1)S(1)}, bf16[2,24,4,128,128]{4,3,2,1,0:T(8,128)(2,1)}, u32[]{:S(2)}) copy-start(bf16[2,24,4,128,128]{4,3,2,1,0:T(8,128)(2,1)} %explicit_ref.5) | copy-start | bytes 18874372
  57.1 2.8 %copy-start.4 = (bf16[2,24,4,128,128]{4,3,2,1,0:T(8,128)(2,1)S(1)}, bf16[2,24,4,128,128]{4,3,2,1,0:T(8,128)(2,1)}, u32[]{:S(2)}) copy-start(bf16[2,24,4,128,128]{4,3,2,1,0:T(8,128)(2,1)} %implicit_ref.3) | copy-start | bytes 18874372

commit v2 on v1

v2 whole, which is shorter than its diff:
```python
import functools

import jax
import jax.numpy as jnp
from jax import lax
from jax.experimental import pallas as pl
from jax.experimental.pallas import tpu as pltpu
from jax.sharding import PartitionSpec as P

REACH = 2
DAYS = 30
STEPS = 2
LOW = 2 * REACH
HIGH = 2 * (REACH - 1)
F32 = jnp.float32
BF16 = jnp.bfloat16
MIB = 1 << 20
SIDE = 4
NT = (((1,), (1,)), ((), ()))


def split_store(ref, where, value):
    half = value.shape[0]
    high = value.astype(BF16)
    ref[where, 0:half, :] = high
    ref[where, half : 2 * half, :] = (value - high.astype(F32)).astype(BF16)


def coefficients(month_ref, weight_ref, step):
    weight = weight_ref[step].astype(F32) * (1.0 / DAYS)
    straight = month_ref[0] == 0
    return (
        jnp.where(straight, 1.0 - weight, weight),
        jnp.where(straight, weight, 1.0 - weight),
    )


def combine(product, coef):
    block = product.shape[1] // 2
    half = product.shape[0] // 2
    mixed = coef[0] * product[:, :block] + coef[1] * product[:, block:]
    return mixed[:half] + mixed[half:]


def column(total, origin_ref, cols_ref, count_ref, row, r, spare):
    at = cols_ref[r, row] - origin_ref[0] * cols_ref.shape[1] + LOW
    at = jnp.where(at < 0, at + total, at)
    at = jnp.where(at >= total, at - total, at)
    return jnp.where(r < count_ref[row], at, spare)


def own_row(values_ref, blocks_ref, tables, row, shift, coef):
    width = blocks_ref.shape[2]
    spare = blocks_ref.shape[1] + LOW + HIGH
    left = jnp.concatenate(
        [values_ref[column(*tables, row, r, spare) - shift] for r in range(width)], axis=1
    )
    right = jnp.concatenate(
        [
            jnp.concatenate([blocks_ref[m, row, r] for r in range(width)], axis=1)
            for m in range(2)
        ],
        axis=0,
    )
    product = lax.dot_general(left, right, NT, preferred_element_type=F32)
    return combine(product, coef)


def edge_row(values_ref, edge_ref, row, first, coef):
    width = edge_ref.shape[2]
    left = jnp.concatenate([values_ref[first + d] for d in range(width)], axis=1)
    right = jnp.concatenate(
        [
            jnp.concatenate([edge_ref[m, row, d].astype(BF16) for d in range(width)], axis=1)
            for m in range(2)
        ],
        axis=0,
    )
    product = lax.dot_general(left, right, NT, preferred_element_type=F32)
    return combine(product, coef)


def prepare_source(side, part, place, mix_ref, bias_ref, rate_ref, mixing_ref, bias_out_ref, rate_out_ref):
    size = mix_ref.shape[0]
    mine = size // (side * side)
    at = lax.broadcasted_iota(jnp.int32, (size, size), 0)
    wanted = lax.broadcasted_iota(jnp.int32, (size, size), 1)
    outer, inner = at // (mine * side), lax.rem(at // mine, side)
    even = lax.rem(part, 2) == 0
    y = lax.rem(place // side + jnp.where(even, outer, inner), side)
    x = lax.rem(lax.rem(place, side) + jnp.where(even, inner, outer), side)
    chosen = (y * side + x) * mine + lax.rem(at, mine) == wanted
    pick = jnp.where(chosen, 1.0, 0.0).astype(BF16)
    mix = mix_ref[...]
    high = mix.astype(BF16)
    low = (mix - high.astype(F32)).astype(BF16)
    tiles = []
    for piece in (high, low):
        rows = lax.dot_general(
            pick, piece, (((1,), (0,)), ((), ())), preferred_element_type=F32
        ).astype(BF16)
        tiles.append(lax.dot_general(rows, pick, NT, preferred_element_type=F32).astype(BF16))
    tile = jnp.concatenate(tiles, axis=0)
    mixing_ref[...] = jnp.concatenate([tile, tile], axis=1)
    for source_ref, target_ref, scale in ((bias_ref, bias_out_ref, 1.0), (rate_ref, rate_out_ref, 0.5)):
        column = jnp.sum(jnp.where(chosen, source_ref[...], 0.0), axis=1, keepdims=True)
        target_ref[...] = jnp.broadcast_to(scale * column, target_ref.shape)


def exchanged(value):
    mine = value.shape[0] // (SIDE * SIDE)
    at = lambda a, b: (a * SIDE + b) * mine
    return jnp.concatenate(
        [value[at(b, a) : at(b, a) + mine] for a in range(SIDE) for b in range(SIDE)], axis=0
    )


def half_source(values, mixing, bias, rate):
    both = lax.dot_general(
        mixing, values, (((1,), (0,)), ((), ())), preferred_element_type=F32
    )
    half = both.shape[0] // 2
    inner = both[:half] + both[half:] + bias
    return rate * inner * jnp.exp(-0.125 * inner * inner)


def edges_kernel(
    total, side, origin_ref, place_ref, cols_ref, count_ref, low_ref, high_ref,
    mix_ref, bias_ref, rate_ref,
    to_right_ref, to_left_ref, mixing_ref, bias_out_ref, rate_out_ref,
):
    width, rows = cols_ref.shape
    for source_ref, target_ref, start in (
        (low_ref, to_right_ref, rows - REACH),
        (high_ref, to_left_ref, 0),
    ):
        for row in range(source_ref.shape[1]):
            n = start + row
            for d in range(width):
                wanted = origin_ref[0] * rows + n + d - REACH
                wanted = jnp.where(wanted < 0, wanted + total, wanted)
                wanted = jnp.where(wanted >= total, wanted - total, wanted)
                slot = jnp.int32(0)
                scale = jnp.float32(0.0)
                for r in range(width):
                    hit = jnp.logical_and(cols_ref[r, n] == wanted, r < count_ref[n])
                    slot = jnp.where(hit, r, slot)
                    scale = jnp.where(hit, 1.0, scale)
                for m in range(2):
                    target_ref[m, row, d] = source_ref[m, row, slot].astype(F32) * scale
    prepare_source(
        side, origin_ref[0], place_ref[0], mix_ref, bias_ref, rate_ref, mixing_ref, bias_out_ref, rate_out_ref
    )


def pack_edges(explicit_blocks, scalars, source, total, side):
    months, rows, width, block, _ = explicit_blocks.shape
    size = source[0].shape[0]
    spec = lambda count, at: pl.BlockSpec(
        (months, count, width, block, block), lambda i: (0, at, 0, 0, 0)
    )
    smem = pl.BlockSpec(memory_space=pltpu.SMEM)
    vmem = pl.BlockSpec(memory_space=pltpu.VMEM)
    shape = lambda count: jax.ShapeDtypeStruct((months, count, width, block, block), F32)
    return pl.pallas_call(
        functools.partial(edges_kernel, total, side),
        grid=(1,),
        in_specs=[smem] * 4
        + [spec(REACH, rows // REACH - 1), spec(REACH - 1, 0)]
        + [vmem] * 3,
        out_specs=[spec(REACH, 0), spec(REACH - 1, 0)] + [vmem] * 3,
        out_shape=[
            shape(REACH),
            shape(REACH - 1),
            jax.ShapeDtypeStruct((2 * size, 2 * size), BF16),
            jax.ShapeDtypeStruct((size, block), F32),
            jax.ShapeDtypeStruct((size, block), F32),
        ],
        compiler_params=pltpu.CompilerParams(vmem_limit_bytes=56 * MIB),
        name="edges",
    )(*scalars, explicit_blocks, explicit_blocks, *source)


def load_kernel(explicit_ref, implicit_ref, explicit_out_ref, implicit_out_ref, sems):
    chunks = sems.shape[1]
    copies = []
    for k, (source, target) in enumerate(
        ((explicit_ref, explicit_out_ref), (implicit_ref, implicit_out_ref))
    ):
        step = source.shape[1] // chunks
        for c in range(chunks):
            at = pl.ds(c * step, step)
            copies.append(
                pltpu.make_async_copy(source.at[:, at], target.at[:, at], sems.at[k, c])
            )
    for copy in copies:
        copy.start()
    for copy in copies:
        copy.wait()


def load(explicit_blocks, implicit_blocks):
    hbm = pl.BlockSpec(memory_space=pl.ANY)
    vmem = pl.BlockSpec(memory_space=pltpu.VMEM)
    return pl.pallas_call(
        load_kernel,
        in_specs=[hbm, hbm],
        out_specs=[vmem, vmem],
        out_shape=[
            pltpu.VMEM(explicit_blocks.shape, explicit_blocks.dtype),
            pltpu.VMEM(implicit_blocks.shape, implicit_blocks.dtype),
        ],
        scratch_shapes=[pltpu.SemaphoreType.DMA((2, 4))],
        compiler_params=pltpu.CompilerParams(vmem_limit_bytes=MIB),
        cost_estimate=pl.CostEstimate(flops=0, bytes_accessed=24 * MIB, transcendentals=0),
        name="load",
    )(explicit_blocks, implicit_blocks)


def first_kernel(
    total, origin_ref, cols_ref, count_ref, month_ref, weight_ref, explicit_ref, implicit_ref,
    near_ref, next_ref, far_ref, back_ref, left_ref, right_ref, mixing_ref, bias_ref, rate_ref,
    low_ref, high_ref, field_out_ref, values_ref, middle_ref,
):
    coef = coefficients(month_ref, weight_ref, 0)
    tables = (total, origin_ref, cols_ref, count_ref)
    rows = explicit_ref.shape[1]
    block = explicit_ref.shape[-1]
    tracers = bias_ref.shape[0]
    ext = rows + LOW + HIGH
    share = near_ref.shape[0] // ext
    zero = jnp.zeros((2 * tracers, block), BF16)
    values_ref[ext] = zero
    middle_ref[ext - REACH] = zero
    for b in range(ext):
        parts = [
            ref[pl.ds(b, share, stride=ext), :] for ref in (near_ref, next_ref, far_ref, back_ref)
        ]
        split_store(values_ref, b, jnp.concatenate(parts, axis=0))
    mixing, bias, rate = mixing_ref[...], bias_ref[...], rate_ref[...]

    def finish(frame, product):
        source = half_source(values_ref[frame + REACH], mixing, bias, rate)
        split_store(middle_ref, frame, product + source)

    for row in range(REACH):
        finish(row, edge_row(values_ref, left_ref, row, row, coef))
    for row in range(REACH - 1):
        frame = rows + REACH + row
        finish(frame, edge_row(values_ref, right_ref, row, frame, coef))
    for row in range(rows):
        finish(row + REACH, own_row(values_ref, explicit_ref, tables, row, 0, coef))

    for row in [*range(rows - LOW, rows), *range(rows - LOW)]:
        result = own_row(middle_ref, implicit_ref, tables, row, REACH, coef)
        split_store(field_out_ref, row, result)
        if row >= rows - LOW:
            at = row - (rows - LOW)
            low_ref[:, at * block : (at + 1) * block] = result
        if row < HIGH:
            high_ref[:, row * block : (row + 1) * block] = result


def inner_kernel(
    total, origin_ref, cols_ref, count_ref, month_ref, weight_ref, field_ref, explicit_ref, mixing_ref, bias_ref, rate_ref,
    middle_ref, values_ref,
):
    coef = coefficients(month_ref, weight_ref, 1)
    tables = (total, origin_ref, cols_ref, count_ref)
    rows = explicit_ref.shape[1]
    values_ref[LOW : LOW + rows] = field_ref[...]
    values_ref[rows + LOW + HIGH] = jnp.zeros(values_ref.shape[1:], BF16)
    mixing, bias, rate = mixing_ref[...], bias_ref[...], rate_ref[...]

    def explicit_row(row, carry):
        product = own_row(values_ref, explicit_ref, tables, row, 0, coef)
        source = half_source(values_ref[row + LOW], mixing, bias, rate)
        split_store(middle_ref, row, product + source)
        return carry

    for row in range(REACH, rows - REACH + 1):
        explicit_row(row, 0)


def last_kernel(
    total, origin_ref, cols_ref, count_ref, month_ref, weight_ref, low_in_ref, high_in_ref, field_ref, middle_in_ref,
    explicit_ref, implicit_ref, left_ref, right_ref, mixing_ref, bias_ref, rate_ref,
    out_ref, values_ref, middle_ref, result_ref,
):
    coef = coefficients(month_ref, weight_ref, 1)
    tables = (total, origin_ref, cols_ref, count_ref)
    rows = explicit_ref.shape[1]
    block = explicit_ref.shape[-1]
    tracers = bias_ref.shape[0]
    ext = rows + LOW + HIGH
    zero = jnp.zeros((2 * tracers, block), BF16)
    values_ref[ext] = zero
    middle_ref[ext - REACH] = zero
    values_ref[LOW : LOW + rows] = field_ref[...]
    middle_ref[2 * REACH : rows + 1] = middle_in_ref[REACH : rows - REACH + 1]
    for b in range(LOW):
        split_store(values_ref, b, exchanged(low_in_ref[:, b * block : (b + 1) * block]))
    for b in range(HIGH):
        value = exchanged(high_in_ref[:, b * block : (b + 1) * block])
        split_store(values_ref, LOW + rows + b, value)
    mixing, bias, rate = mixing_ref[...], bias_ref[...], rate_ref[...]

    def finish(frame, product):
        source = half_source(values_ref[frame + REACH], mixing, bias, rate)
        split_store(middle_ref, frame, product + source)

    for row in range(REACH):
        finish(row, edge_row(values_ref, left_ref, row, row, coef))
    for row in range(REACH - 1):
        frame = rows + REACH + row
        finish(frame, edge_row(values_ref, right_ref, row, frame, coef))
    for row in [*range(REACH), *range(rows - REACH + 1, rows)]:
        finish(row + REACH, own_row(values_ref, explicit_ref, tables, row, 0, coef))

    for row in range(rows):
        result_ref[:, row * block : (row + 1) * block] = own_row(
            middle_ref, implicit_ref, tables, row, REACH, coef
        )
    out_ref[...] = result_ref[: out_ref.shape[0], :]


def call(kernel, name, smem_count, hbm_count, args, outs, scratch, flops, limit):
    smem = pl.BlockSpec(memory_space=pltpu.SMEM)
    vmem = pl.BlockSpec(memory_space=pltpu.VMEM)
    hbm = pl.BlockSpec(memory_space=pltpu.HBM)
    return pl.pallas_call(
        kernel,
        in_specs=[smem] * smem_count
        + [hbm] * hbm_count
        + [vmem] * (len(args) - smem_count - hbm_count),
        out_specs=[vmem] * len(outs),
        out_shape=outs,
        scratch_shapes=scratch,
        compiler_params=pltpu.CompilerParams(vmem_limit_bytes=limit * MIB),
        cost_estimate=pl.CostEstimate(flops=flops, bytes_accessed=8 * MIB, transcendentals=0),
        name=name,
    )(*args)


def per_device(
    tracers,
    explicit_blocks,
    implicit_blocks,
    column_blocks,
    block_count,
    month_pair,
    weight_num,
    source_mix,
    source_bias,
    source_rate,
):
    rows, width = column_blocks.shape
    block = explicit_blocks.shape[-1]
    parts = lax.axis_size("pts")
    groups = lax.axis_size("trc")
    mine = tracers.shape[0]
    total = source_mix.shape[0]
    ext = rows + LOW + HIGH
    forward = [(i, (i + 1) % parts) for i in range(parts)]
    backward = [(target, source) for source, target in forward]

    low = lax.ppermute(tracers, "pts", forward)[:, -LOW * block :]
    high = lax.ppermute(tracers, "pts", backward)[:, : HIGH * block]
    origin = lax.axis_index("pts").astype(jnp.int32).reshape(1)
    place = lax.axis_index("trc").astype(jnp.int32).reshape(1)
    scalars = (origin, column_blocks.T, block_count, month_pair, weight_num)
    to_right, to_left, *source = pack_edges(
        explicit_blocks,
        (origin, place, column_blocks.T, block_count),
        (source_mix, source_bias[None], source_rate[None]),
        rows * parts,
        SIDE,
    )
    low, high, to_right, to_left = lax.optimization_barrier((low, high, to_right, to_left))
    extended = jnp.concatenate([low, tracers, high], axis=1).reshape(mine * ext, block)
    both = ("pts", "trc")

    def along(stage, k):
        moves = []
        for p in range(parts):
            for t in range(groups):
                y, x = divmod(t, SIDE)
                if (p + stage) % 2 == 0:
                    source_at = y * SIDE + (x + k) % SIDE
                else:
                    source_at = (y + k) % SIDE * SIDE + x
                moves.append((p * groups + source_at, p * groups + t))
        return moves

    line = jnp.concatenate(
        [extended] + [lax.ppermute(extended, both, along(0, k)) for k in range(1, SIDE)]
    )
    line, explicit_blocks, implicit_blocks = lax.optimization_barrier(
        (line, explicit_blocks, implicit_blocks)
    )
    gathered = [line] + [lax.ppermute(line, both, along(1, k)) for k in range(1, SIDE)]
    explicit_blocks, implicit_blocks = load(explicit_blocks, implicit_blocks)
    left = lax.ppermute(to_right, "pts", forward)
    right = lax.ppermute(to_left, "pts", backward)

    shape = jax.ShapeDtypeStruct
    stack = lambda count: pltpu.VMEM((count, 2 * total, block), BF16)
    one = 2 * 2 * total * 2 * block * width * block
    low, high, field = call(
        functools.partial(first_kernel, rows * parts), "first", 5, 0,
        (*scalars, explicit_blocks, implicit_blocks, *gathered, left, right, *source),
        [
            shape((total, LOW * block), F32),
            shape((total, HIGH * block), F32),
            shape((rows, 2 * total, block), BF16),
        ],
        [
            stack(ext + 1),
            stack(ext - REACH + 1),
        ],
        51 * one, 12,
    )
    low = lax.ppermute(low, "pts", forward)
    high = lax.ppermute(high, "pts", backward)
    (middle,) = call(
        functools.partial(inner_kernel, rows * parts), "inner", 5, 0,
        (*scalars, field, explicit_blocks, *source),
        [shape((rows, 2 * total, block), BF16)],
        [stack(ext + 1)],
        21 * one, 12,
    )
    (advanced,) = call(
        functools.partial(last_kernel, rows * parts), "last", 5, 0,
        (
            *scalars, low, high, field, middle, explicit_blocks, implicit_blocks,
            left, right, *source,
        ),
        [shape((mine, rows * block), F32)],
        [stack(ext + 1), stack(ext - REACH + 1), pltpu.VMEM((total, rows * block), F32)],
        30 * one, 12,
    )
    return advanced


def solution(mesh):
    in_specs = (
        P("trc", "pts"),
        P(None, "pts", None, None, None),
        P(None, "pts", None, None, None),
        P("pts", None),
        P("pts"),
        P(),
        P(),
        P(),
        P(),
        P(),
    )
    out_specs = P("trc", "pts")
    return jax.shard_map(
        per_device, mesh=mesh, in_specs=in_specs, out_specs=out_specs, check_vma=False
    )
```

time: 64.5 us -> 48.1 us (0.75)
  the two profiles are of different devices: /device:TPU:65 before, /device:TPU:97 now
where the time goes in v2:
time: 48.1 us; the launch traced here: 48 us
  starting transfers between devices  19.7 us (41%)
  Pallas kernels  15.5 us (32%)
  waiting for transfers between devices  6.9 us (14%)
  local copies, waits for them, and re-layouts  5.64 us (12%)
    pallas_call x3, Pallas kernels, call(): pl.pallas_call(kernel, in_specs=[smem] * smem_count + [hbm] * hbm_count +...  11.9 us
    unnamed x20, local copies, waits for them, and re-layouts  5.61 us
    ppermute x1, starting transfers between devices, per_device(): low = lax.ppermute(low, 'pts', forward)  5.57 us
    ppermute x3, starting transfers between devices, per_device(): lax.ppermute(extended, both, along(0, k))  5.06 us
    ppermute x3, starting transfers between devices, per_device(): lax.ppermute(line, both, along(1, k))  4.89 us
    ppermute x1, starting transfers between devices, per_device(): low = lax.ppermute(tracers, 'pts', forward)[:, -LOW * block:]  3.41 us
    pallas_call x1, Pallas kernels, pack_edges(): pl.pallas_call(functools.partial(edges_kernel, total, side), grid=(1,), i...  2.68 us
    ppermute x1, waiting for transfers between devices, per_device(): high = lax.ppermute(high, 'pts', backward)  2.35 us
  transfers between devices with their start and end apart: 12, of which 4 were waited for; matrix products, arithmetic and copies ran while one was open for 0% of the time, Pallas kernels for 13%

profile of v2, /device:TPU:97, one launch (start us, length us, event | category | flops | bytes accessed | tf_op | source)
XLA Modules:
  0.0 48.0 jit_solution(11858369272738189864)
XLA Ops:
  0.0 3.4 %collective-permute-start = (f32[4,3072]{1,0:T(4,128)}, f32[4,3072]{1,0:T(4,128)S(1)}, u32[]{:S(2)}, u32[]{:S(2)}) collective-permute-start(f32[4,3072]{1,0:T(4,128)} %param.10), channel_id=1, source_target_pairs={{0,16},{16,32},{32,48},{48,64},{64,80},{80,96},{96,112},{112,128},... | collective-permute-start | bytes 147464 | tf_op jit(solution)/shard_map/ppermute | solution.py:367
  3.4 0.0 collective-permute-start.1
  3.4 0.0 copy-start.9
  3.4 2.7 %edges.1 = (f32[2,2,4,128,128]{4,3,2,1,0:T(8,128)}, f32[2,1,4,128,128]{4,3,2,1,0:T(8,128)}, bf16[128,128]{1,0:T(8,128)(2,1)}, f32[64,128]{1,0:T(8,128)}, f32[64,128]{1,0:T(8,128)}) custom-call(s32[1]{0:T(128)} %bitcast.origin_ref, s32[1]{0:T(128)} %bitcast.2.place_ref, s32[4,24]{1,0:T(4,128)} %bitcast.5, s32[24]{0:T(128)} %count_ref.7, ...), custom_call_target="tpu_custom_call" | custom-call | tf_op jit(solution)/shard_map/edges/pallas_call | solution.py:165
  6.1 0.0 collective-permute-done
  6.1 2.2 %collective-permute-done.1 = f32[4,3072]{1,0:T(4,128)S(1)} collective-permute-done((f32[4,3072]{1,0:T(4,128)}, f32[4,3072]{1,0:T(4,128)S(1)}, u32[]{:S(2)}, u32[]{:S(2)}) %collective-permute-start.1) | collective-permute-done | bytes 49184 | tf_op jit(solution)/shard_map/ppermute | solution.py:368
  8.3 0.7 %collective-permute-start.8 = (f32[2,2,4,128,128]{4,3,2,1,0:T(8,128)}, f32[2,2,4,128,128]{4,3,2,1,0:T(8,128)S(1)}, u32[]{:S(2)}, u32[]{:S(2)}) collective-permute-start(f32[2,2,4,128,128]{4,3,2,1,0:T(8,128)} %get-tuple-element.31), channel_id=1, source_target_pairs={{0,16},{16,32},{32,48},{48,64},{64,80},{80,96},{96,112},{112,128},... | collective-permute-start | bytes 3145736 | tf_op jit(solution)/shard_map/ppermute | solution.py:403
  9.1 0.0 collective-permute-start.9
  9.1 0.0 copy-done.9
  9.2 1.4 %collective-permute-start.4 = (f32[120,128]{1,0:T(8,128)S(1)}, f32[120,128]{1,0:T(8,128)S(1)}, u32[]{:S(2)}, u32[]{:S(2)}) collective-permute-start(f32[120,128]{1,0:T(8,128)S(1)} %reshape.11), channel_id=1, source_target_pairs={{3,0},{0,1},{1,2},{2,3},{7,4},{4,5},{5,6},{6,7},{11,8},{8,9},{9,10... | collective-permute-start | bytes 184328 | tf_op jit(solution)/shard_map/ppermute | solution.py:396
  10.5 2.6 %collective-permute-start.3 = (f32[120,128]{1,0:T(8,128)S(1)}, f32[120,128]{1,0:T(8,128)S(1)}, u32[]{:S(2)}, u32[]{:S(2)}) collective-permute-start(f32[120,128]{1,0:T(8,128)S(1)} %reshape.11), channel_id=1, source_target_pairs={{2,0},{3,1},{0,2},{1,3},{6,4},{7,5},{4,6},{5,7},{10,8},{11,9},{8,1... | collective-permute-start | bytes 184328 | tf_op jit(solution)/shard_map/ppermute | solution.py:396
  13.1 1.1 %collective-permute-start.2 = (f32[120,128]{1,0:T(8,128)S(1)}, f32[120,128]{1,0:T(8,128)S(1)}, u32[]{:S(2)}, u32[]{:S(2)}) collective-permute-start(f32[120,128]{1,0:T(8,128)S(1)} %reshape.11), channel_id=1, source_target_pairs={{1,0},{2,1},{3,2},{0,3},{5,4},{6,5},{7,6},{4,7},{9,8},{10,9},{11,1... | collective-permute-start | bytes 184328 | tf_op jit(solution)/shard_map/ppermute | solution.py:396
  14.2 0.0 collective-permute-done.4
  14.2 1.5 %collective-permute-done.3 = f32[120,128]{1,0:T(8,128)S(1)} collective-permute-done((f32[120,128]{1,0:T(8,128)S(1)}, f32[120,128]{1,0:T(8,128)S(1)}, u32[]{:S(2)}, u32[]{:S(2)}) %collective-permute-start.3) | collective-permute-done | bytes 61472 | tf_op jit(solution)/shard_map/ppermute | solution.py:396
  15.7 0.8 %collective-permute-done.2 = f32[120,128]{1,0:T(8,128)S(1)} collective-permute-done((f32[120,128]{1,0:T(8,128)S(1)}, f32[120,128]{1,0:T(8,128)S(1)}, u32[]{:S(2)}, u32[]{:S(2)}) %collective-permute-start.2) | collective-permute-done | bytes 61472 | tf_op jit(solution)/shard_map/ppermute | solution.py:396
  16.5 0.0 copy-start.2
  16.5 0.0 copy-start.4
  16.5 0.0 copy-start.5
  16.5 0.0 copy-start.6
  16.5 0.0 copy-start.7
  16.6 0.0 copy-start.8
  16.6 1.3 %collective-permute-start.7 = (f32[480,128]{1,0:T(8,128)S(1)}, f32[480,128]{1,0:T(8,128)S(1)}, u32[]{:S(2)}, u32[]{:S(2)}) collective-permute-start(f32[480,128]{1,0:T(8,128)S(1)} %pad_maximum_fusion.near_ref), channel_id=1, source_target_pairs={{12,0},{13,1},{14,2},{15,3},{0,4},{1,5},{2,6},{3,7},{4,8},{5,9},{6... | collective-permute-start | bytes 737288 | tf_op jit(solution)/shard_map/ppermute | solution.py:401
  17.9 2.5 %collective-permute-start.6 = (f32[480,128]{1,0:T(8,128)S(1)}, f32[480,128]{1,0:T(8,128)S(1)}, u32[]{:S(2)}, u32[]{:S(2)}) collective-permute-start(f32[480,128]{1,0:T(8,128)S(1)} %pad_maximum_fusion.near_ref), channel_id=1, source_target_pairs={{8,0},{9,1},{10,2},{11,3},{12,4},{13,5},{14,6},{15,7},{0,8},{1,9},... | collective-permute-start | bytes 737288 | tf_op jit(solution)/shard_map/ppermute | solution.py:401
  20.3 1.2 %collective-permute-start.5 = (f32[480,128]{1,0:T(8,128)S(1)}, f32[480,128]{1,0:T(8,128)S(1)}, u32[]{:S(2)}, u32[]{:S(2)}) collective-permute-start(f32[480,128]{1,0:T(8,128)S(1)} %pad_maximum_fusion.near_ref), channel_id=1, source_target_pairs={{4,0},{5,1},{6,2},{7,3},{8,4},{9,5},{10,6},{11,7},{12,8},{13,9},{1... | collective-permute-start | bytes 737288 | tf_op jit(solution)/shard_map/ppermute | solution.py:401
  21.5 0.0 copy-start
  21.5 2.8 %copy-done = bf16[2,24,4,128,128]{4,3,2,1,0:T(8,128)(2,1)S(1)} copy-done((bf16[2,24,4,128,128]{4,3,2,1,0:T(8,128)(2,1)S(1)}, bf16[2,24,4,128,128]{4,3,2,1,0:T(8,128)(2,1)}, u32[]{:S(2)}) %copy-start) | copy-done | bytes 6291480
  24.3 0.0 copy-start.1
  24.3 2.8 %copy-done.1 = bf16[2,24,4,128,128]{4,3,2,1,0:T(8,128)(2,1)S(1)} copy-done((bf16[2,24,4,128,128]{4,3,2,1,0:T(8,128)(2,1)S(1)}, bf16[2,24,4,128,128]{4,3,2,1,0:T(8,128)(2,1)}, u32[]{:S(2)}) %copy-start.1) | copy-done | bytes 6291480
  27.1 0.9 %load.1 = (bf16[2,24,4,128,128]{4,3,2,1,0:T(8,128)(2,1)S(1)}, bf16[2,24,4,128,128]{4,3,2,1,0:T(8,128)(2,1)S(1)}) custom-call(bf16[2,24,4,128,128]{4,3,2,1,0:T(8,128)(2,1)S(1)} %copy-done, bf16[2,24,4,128,128]{4,3,2,1,0:T(8,128)(2,1)S(1)} %copy-done.1), custom_call_target="tpu_custom_call" | custom-call | bytes 25165824 | tf_op jit(solution)/shard_map/load/pallas_call | solution.py:205
  28.0 0.0 collective-permute-done.7.back_ref
  28.0 0.0 collective-permute-done.6.far_ref
  28.0 0.0 collective-permute-done.5.next_ref
  28.0 0.0 collective-permute-done.9.right_ref
  28.0 0.0 collective-permute-done.8.left_ref
  28.0 0.0 copy-done.2
  28.0 0.0 copy-done.3
  28.1 0.0 copy-done.4
  28.1 0.0 copy-done.5
  28.1 0.0 copy-done.6
  28.1 0.0 copy-done.7
  28.1 0.0 copy-done.8
  28.1 5.4 %first.1 = (f32[64,512]{1,0:T(8,128)S(1)}, f32[64,256]{1,0:T(8,128)S(1)}, bf16[24,128,128]{2,1,0:T(8,128)(2,1)S(1)}) custom-call(s32[1]{0:T(128)} %bitcast.origin_ref, s32[4,24]{1,0:T(4,128)S(1)} %bitcast.6, s32[24]{0:T(128)S(1)} %copy-done.6, s32[2]{0:T(128)S(1)} %copy-done.7, s32[2]{0:T(128)S(1)} %copy-done.8, ...), custom_call_target="tpu_custom_call" | custom-call | flops 1711276032 | bytes 8388608 | tf_op jit(solution)/shard_map/first/pallas_call | solution.py:331
  33.5 5.6 %collective-permute-start.10 = (f32[64,512]{1,0:T(8,128)S(1)}, f32[64,512]{1,0:T(8,128)S(1)}, u32[]{:S(2)}, u32[]{:S(2)}) collective-permute-start(f32[64,512]{1,0:T(8,128)S(1)} %get-tuple-element.36), channel_id=1, source_target_pairs={{0,16},{16,32},{32,48},{48,64},{64,80},{80,96},{96,112},{112,128},... | collective-permute-start | bytes 393224 | tf_op jit(solution)/shard_map/ppermute | solution.py:423
  39.0 0.0 collective-permute-start.11
  39.0 2.5 %inner.1.middle_in_ref = bf16[24,128,128]{2,1,0:T(8,128)(2,1)S(1)} custom-call(s32[1]{0:T(128)} %bitcast.origin_ref, s32[4,24]{1,0:T(4,128)S(1)} %bitcast.7, s32[24]{0:T(128)S(1)} %copy-done.6, s32[2]{0:T(128)S(1)} %copy-done.7, s32[2]{0:T(128)S(1)} %copy-done.8, bf16[24,128,128]{2,1,0:T(8,128)(2,1)S(1)} %get-tuple-element.38.field_ref, ...), custom_call_target="tpu_custom_call" | custom-call | flops 704643072 | bytes 8388608 | tf_op jit(solution)/shard_map/inner/pallas_call | solution.py:331
  41.6 2.3 %collective-permute-done.11.high_in_ref = f32[64,256]{1,0:T(8,128)S(1)} collective-permute-done((f32[64,256]{1,0:T(8,128)S(1)}, f32[64,256]{1,0:T(8,128)S(1)}, u32[]{:S(2)}, u32[]{:S(2)}) %collective-permute-start.11) | collective-permute-done | bytes 65568 | tf_op jit(solution)/shard_map/ppermute | solution.py:424
  43.9 0.0 collective-permute-done.10.low_in_ref
  43.9 4.0 %last.1 = f32[4,3072]{1,0:T(4,128)} custom-call(s32[1]{0:T(128)} %bitcast.origin_ref, s32[4,24]{1,0:T(4,128)S(1)} %bitcast.8, s32[24]{0:T(128)S(1)} %copy-done.6, s32[2]{0:T(128)S(1)} %copy-done.7, s32[2]{0:T(128)S(1)} %copy-done.8, f32[64,512]{1,0:T(8,128)S(1)} %collective-permute-done.10.low_in_ref, f32[64,256]{1,0:T(8,128)S(1)} %collective-permute-done.11.high_in_ref, ...), custom_call_target="tpu_custom_call" | custom-call | flops 1006632960 | bytes 8388608 | tf_op jit(solution)/shard_map/last/pallas_call | solution.py:331
  (6 shorter events, 0.1 us)
Async XLA Ops:
  0.0 6.1 %collective-permute-start = (f32[4,3072]{1,0:T(4,128)}, f32[4,3072]{1,0:T(4,128)S(1)}, u32[]{:S(2)}, u32[]{:S(2)}) collective-permute-start(f32[4,3072]{1,0:T(4,128)} %param.10), channel_id=1, source_target_pairs={{0,16},{16,32},{32,48},{48,64},{64,80},{80,96},{96,112},{112,128},... | collective-permute-start | bytes 147464 | tf_op jit(solution)/shard_map/ppermute | solution.py:367
  3.4 4.9 %collective-permute-start.1 = (f32[4,3072]{1,0:T(4,128)}, f32[4,3072]{1,0:T(4,128)S(1)}, u32[]{:S(2)}, u32[]{:S(2)}) collective-permute-start(f32[4,3072]{1,0:T(4,128)} %param.10), channel_id=1, source_target_pairs={{16,0},{32,16},{48,32},{64,48},{80,64},{96,80},{112,96},{128,112},... | collective-permute-start | bytes 147464 | tf_op jit(solution)/shard_map/ppermute | solution.py:368
  3.4 5.7 %copy-start.9 = (f32[4,3072]{1,0:T(4,128)S(1)}, f32[4,3072]{1,0:T(4,128)}, u32[]{:S(2)}) copy-start(f32[4,3072]{1,0:T(4,128)} %param.10) | copy-start | bytes 147460
  8.3 19.7 %collective-permute-start.8 = (f32[2,2,4,128,128]{4,3,2,1,0:T(8,128)}, f32[2,2,4,128,128]{4,3,2,1,0:T(8,128)S(1)}, u32[]{:S(2)}, u32[]{:S(2)}) collective-permute-start(f32[2,2,4,128,128]{4,3,2,1,0:T(8,128)} %get-tuple-element.31), channel_id=1, source_target_pairs={{0,16},{16,32},{32,48},{48,64},{64,80},{80,96},{96,112},{112,128},... | collective-permute-start | bytes 3145736 | tf_op jit(solution)/shard_map/ppermute | solution.py:403
  9.1 18.9 %collective-permute-start.9 = (f32[2,1,4,128,128]{4,3,2,1,0:T(8,128)}, f32[2,1,4,128,128]{4,3,2,1,0:T(8,128)S(1)}, u32[]{:S(2)}, u32[]{:S(2)}) collective-permute-start(f32[2,1,4,128,128]{4,3,2,1,0:T(8,128)} %get-tuple-element.32), channel_id=1, source_target_pairs={{16,0},{32,16},{48,32},{64,48},{80,64},{96,80},{112,96},{128,112},... | collective-permute-start | bytes 1572872 | tf_op jit(solution)/shard_map/ppermute | solution.py:404
  9.2 5.1 %collective-permute-start.4 = (f32[120,128]{1,0:T(8,128)S(1)}, f32[120,128]{1,0:T(8,128)S(1)}, u32[]{:S(2)}, u32[]{:S(2)}) collective-permute-start(f32[120,128]{1,0:T(8,128)S(1)} %reshape.11), channel_id=1, source_target_pairs={{3,0},{0,1},{1,2},{2,3},{7,4},{4,5},{5,6},{6,7},{11,8},{8,9},{9,10... | collective-permute-start | bytes 184328 | tf_op jit(solution)/shard_map/ppermute | solution.py:396
  10.5 5.2 %collective-permute-start.3 = (f32[120,128]{1,0:T(8,128)S(1)}, f32[120,128]{1,0:T(8,128)S(1)}, u32[]{:S(2)}, u32[]{:S(2)}) collective-permute-start(f32[120,128]{1,0:T(8,128)S(1)} %reshape.11), channel_id=1, source_target_pairs={{2,0},{3,1},{0,2},{1,3},{6,4},{7,5},{4,6},{5,7},{10,8},{11,9},{8,1... | collective-permute-start | bytes 184328 | tf_op jit(solution)/shard_map/ppermute | solution.py:396
  13.1 3.4 %collective-permute-start.2 = (f32[120,128]{1,0:T(8,128)S(1)}, f32[120,128]{1,0:T(8,128)S(1)}, u32[]{:S(2)}, u32[]{:S(2)}) collective-permute-start(f32[120,128]{1,0:T(8,128)S(1)} %reshape.11), channel_id=1, source_target_pairs={{1,0},{2,1},{3,2},{0,3},{5,4},{6,5},{7,6},{4,7},{9,8},{10,9},{11,1... | collective-permute-start | bytes 184328 | tf_op jit(solution)/shard_map/ppermute | solution.py:396
  16.5 11.5 %copy-start.2 = (bf16[128,128]{1,0:T(8,128)(2,1)S(1)}, bf16[128,128]{1,0:T(8,128)(2,1)}, u32[]{:S(2)}) copy-start(bf16[128,128]{1,0:T(8,128)(2,1)} %get-tuple-element.33.mixing_ref) | copy-start | bytes 98308
  16.5 11.5 %copy-start.3 = (f32[64,128]{1,0:T(8,128)S(1)}, f32[64,128]{1,0:T(8,128)}, u32[]{:S(2)}) copy-start(f32[64,128]{1,0:T(8,128)} %get-tuple-element.34.bias_ref) | copy-start | bytes 98308
  16.5 11.5 %copy-start.4 = (f32[64,128]{1,0:T(8,128)S(1)}, f32[64,128]{1,0:T(8,128)}, u32[]{:S(2)}) copy-start(f32[64,128]{1,0:T(8,128)} %get-tuple-element.35.rate_ref) | copy-start | bytes 98308
  16.5 11.5 %copy-start.5 = (s32[24,4]{0,1:T(4,128)S(1)}, s32[24,4]{0,1:T(4,128)}, u32[]{:S(2)}) copy-start(s32[24,4]{0,1:T(4,128)} %param.13) | copy-start | bytes 1156
  16.5 11.6 %copy-start.6 = (s32[24]{0:T(128)S(1)}, s32[24]{0:T(128)}, u32[]{:S(2)}) copy-start(s32[24]{0:T(128)} %count_ref.7) | copy-start | bytes 292
  16.5 11.5 %copy-start.7 = (s32[2]{0:T(128)S(1)}, s32[2]{0:T(128)}, u32[]{:S(2)}) copy-start(s32[2]{0:T(128)} %month_ref.5) | copy-start | bytes 28
  16.6 11.5 %copy-start.8 = (s32[2]{0:T(128)S(1)}, s32[2]{0:T(128)}, u32[]{:S(2)}) copy-start(s32[2]{0:T(128)} %weight_ref.5) | copy-start | bytes 28
  16.6 11.4 %collective-permute-start.7 = (f32[480,128]{1,0:T(8,128)S(1)}, f32[480,128]{1,0:T(8,128)S(1)}, u32[]{:S(2)}, u32[]{:S(2)}) collective-permute-start(f32[480,128]{1,0:T(8,128)S(1)} %pad_maximum_fusion.near_ref), channel_id=1, source_target_pairs={{12,0},{13,1},{14,2},{15,3},{0,4},{1,5},{2,6},{3,7},{4,8},{5,9},{6... | collective-permute-start | bytes 737288 | tf_op jit(solution)/shard_map/ppermute | solution.py:401
  17.9 10.1 %collective-permute-start.6 = (f32[480,128]{1,0:T(8,128)S(1)}, f32[480,128]{1,0:T(8,128)S(1)}, u32[]{:S(2)}, u32[]{:S(2)}) collective-permute-start(f32[480,128]{1,0:T(8,128)S(1)} %pad_maximum_fusion.near_ref), channel_id=1, source_target_pairs={{8,0},{9,1},{10,2},{11,3},{12,4},{13,5},{14,6},{15,7},{0,8},{1,9},... | collective-permute-start | bytes 737288 | tf_op jit(solution)/shard_map/ppermute | solution.py:401
  20.3 7.7 %collective-permute-start.5 = (f32[480,128]{1,0:T(8,128)S(1)}, f32[480,128]{1,0:T(8,128)S(1)}, u32[]{:S(2)}, u32[]{:S(2)}) collective-permute-start(f32[480,128]{1,0:T(8,128)S(1)} %pad_maximum_fusion.near_ref), channel_id=1, source_target_pairs={{4,0},{5,1},{6,2},{7,3},{8,4},{9,5},{10,6},{11,7},{12,8},{13,9},{1... | collective-permute-start | bytes 737288 | tf_op jit(solution)/shard_map/ppermute | solution.py:401
  21.5 2.8 %copy-start = (bf16[2,24,4,128,128]{4,3,2,1,0:T(8,128)(2,1)S(1)}, bf16[2,24,4,128,128]{4,3,2,1,0:T(8,128)(2,1)}, u32[]{:S(2)}) copy-start(bf16[2,24,4,128,128]{4,3,2,1,0:T(8,128)(2,1)} %explicit_ref) | copy-start | bytes 18874372
  24.3 2.8 %copy-start.1 = (bf16[2,24,4,128,128]{4,3,2,1,0:T(8,128)(2,1)S(1)}, bf16[2,24,4,128,128]{4,3,2,1,0:T(8,128)(2,1)}, u32[]{:S(2)}) copy-start(bf16[2,24,4,128,128]{4,3,2,1,0:T(8,128)(2,1)} %implicit_ref) | copy-start | bytes 18874372
  33.5 10.5 %collective-permute-start.10 = (f32[64,512]{1,0:T(8,128)S(1)}, f32[64,512]{1,0:T(8,128)S(1)}, u32[]{:S(2)}, u32[]{:S(2)}) collective-permute-start(f32[64,512]{1,0:T(8,128)S(1)} %get-tuple-element.36), channel_id=1, source_target_pairs={{0,16},{16,32},{32,48},{48,64},{64,80},{80,96},{96,112},{112,128},... | collective-permute-start | bytes 393224 | tf_op jit(solution)/shard_map/ppermute | solution.py:423
  39.0 4.9 %collective-permute-start.11 = (f32[64,256]{1,0:T(8,128)S(1)}, f32[64,256]{1,0:T(8,128)S(1)}, u32[]{:S(2)}, u32[]{:S(2)}) collective-permute-start(f32[64,256]{1,0:T(8,128)S(1)} %get-tuple-element.37), channel_id=1, source_target_pairs={{16,0},{32,16},{48,32},{64,48},{80,64},{96,80},{112,96},{128,112},... | collective-permute-start | bytes 196616 | tf_op jit(solution)/shard_map/ppermute | solution.py:424

commit v3 on v2

--- a/solution.py
+++ b/solution.py
@@ -211,7 +211,7 @@
             pltpu.VMEM(implicit_blocks.shape, implicit_blocks.dtype),
         ],
         scratch_shapes=[pltpu.SemaphoreType.DMA((2, 4))],
-        compiler_params=pltpu.CompilerParams(vmem_limit_bytes=MIB),
+        compiler_params=pltpu.CompilerParams(vmem_limit_bytes=44 * MIB),
         cost_estimate=pl.CostEstimate(flops=0, bytes_accessed=24 * MIB, transcendentals=0),
         name="load",
     )(explicit_blocks, implicit_blocks)

time: 48.1 us -> 46.5 us (0.967)
  the two profiles are of different devices: /device:TPU:97 before, /device:TPU:16 now
where the time goes in v3:
time: 46.5 us; the launch traced here: 46 us
  starting transfers between devices  19.6 us (42%)
  Pallas kernels  19.1 us (41%)
  waiting for transfers between devices  7.06 us (15%)
    pallas_call x3, Pallas kernels, call(): pl.pallas_call(kernel, in_specs=[smem] * smem_count + [hbm] * hbm_count +...  11.7 us
    ppermute x3, starting transfers between devices, per_device(): lax.ppermute(extended, both, along(0, k))  5.73 us
    ppermute x1, starting transfers between devices, per_device(): high = lax.ppermute(tracers, 'pts', backward)[:, :HIGH * block]  5.3 us
    pallas_call x1, Pallas kernels, load(): pl.pallas_call(load_kernel, in_specs=[hbm, hbm], out_specs=[vmem, vmem],...  4.7 us
    ppermute x3, waiting for transfers between devices, per_device(): lax.ppermute(line, both, along(1, k))  3.69 us
    ppermute x3, waiting for transfers between devices, per_device(): lax.ppermute(extended, both, along(0, k))  3.21 us
    ppermute x1, starting transfers between devices, per_device(): right = lax.ppermute(to_left, 'pts', backward)  2.94 us
    ppermute x1, starting transfers between devices, per_device(): high = lax.ppermute(high, 'pts', backward)  2.94 us
  transfers between devices with their start and end apart: 12, of which 5 were waited for; matrix products, arithmetic and copies ran while one was open for 0% of the time, Pallas kernels for 21%

profile of v3, /device:TPU:16, one launch (start us, length us, event | category | flops | bytes accessed | tf_op | source)
XLA Modules:
  0.0 46.0 jit_solution(8906614252512389834)
XLA Ops:
  0.0 0.0 collective-permute-start
  0.0 5.3 %collective-permute-start.1 = (f32[4,3072]{1,0:T(4,128)}, f32[4,3072]{1,0:T(4,128)S(1)}, u32[]{:S(2)}, u32[]{:S(2)}) collective-permute-start(f32[4,3072]{1,0:T(4,128)} %param.10), channel_id=1, source_target_pairs={{16,0},{32,16},{48,32},{64,48},{80,64},{96,80},{112,96},{128,112},... | collective-permute-start | bytes 147464 | tf_op jit(solution)/shard_map/ppermute | solution.py:368
  5.3 0.0 copy-start.7
  5.3 2.7 %edges.1 = (f32[2,2,4,128,128]{4,3,2,1,0:T(8,128)}, f32[2,1,4,128,128]{4,3,2,1,0:T(8,128)}, bf16[128,128]{1,0:T(8,128)(2,1)}, f32[64,128]{1,0:T(8,128)}, f32[64,128]{1,0:T(8,128)}) custom-call(s32[1]{0:T(128)} %bitcast.origin_ref, s32[1]{0:T(128)} %bitcast.2.place_ref, s32[4,24]{1,0:T(4,128)} %bitcast.5, s32[24]{0:T(128)} %count_ref.7, ...), custom_call_target="tpu_custom_call" | custom-call | tf_op jit(solution)/shard_map/edges/pallas_call | solution.py:165
  8.0 0.0 collective-permute-done
  8.0 0.0 collective-permute-done.1
  8.0 0.0 collective-permute-start.8
  8.0 2.9 %collective-permute-start.9 = (f32[2,1,4,128,128]{4,3,2,1,0:T(8,128)}, f32[2,1,4,128,128]{4,3,2,1,0:T(8,128)S(1)}, u32[]{:S(2)}, u32[]{:S(2)}) collective-permute-start(f32[2,1,4,128,128]{4,3,2,1,0:T(8,128)} %get-tuple-element.32), channel_id=1, source_target_pairs={{16,0},{32,16},{48,32},{64,48},{80,64},{96,80},{112,96},{128,112},... | collective-permute-start | bytes 1572872 | tf_op jit(solution)/shard_map/ppermute | solution.py:404
  11.0 0.0 copy-done.7
  11.0 1.6 %collective-permute-start.4 = (f32[120,128]{1,0:T(8,128)S(1)}, f32[120,128]{1,0:T(8,128)S(1)}, u32[]{:S(2)}, u32[]{:S(2)}) collective-permute-start(f32[120,128]{1,0:T(8,128)S(1)} %reshape.11), channel_id=1, source_target_pairs={{3,0},{0,1},{1,2},{2,3},{7,4},{4,5},{5,6},{6,7},{11,8},{8,9},{9,10... | collective-permute-start | bytes 184328 | tf_op jit(solution)/shard_map/ppermute | solution.py:396
  12.6 2.7 %collective-permute-start.3 = (f32[120,128]{1,0:T(8,128)S(1)}, f32[120,128]{1,0:T(8,128)S(1)}, u32[]{:S(2)}, u32[]{:S(2)}) collective-permute-start(f32[120,128]{1,0:T(8,128)S(1)} %reshape.11), channel_id=1, source_target_pairs={{2,0},{3,1},{0,2},{1,3},{6,4},{7,5},{4,6},{5,7},{10,8},{11,9},{8,1... | collective-permute-start | bytes 184328 | tf_op jit(solution)/shard_map/ppermute | solution.py:396
  15.3 1.4 %collective-permute-start.2 = (f32[120,128]{1,0:T(8,128)S(1)}, f32[120,128]{1,0:T(8,128)S(1)}, u32[]{:S(2)}, u32[]{:S(2)}) collective-permute-start(f32[120,128]{1,0:T(8,128)S(1)} %reshape.11), channel_id=1, source_target_pairs={{1,0},{2,1},{3,2},{0,3},{5,4},{6,5},{7,6},{4,7},{9,8},{10,9},{11,1... | collective-permute-start | bytes 184328 | tf_op jit(solution)/shard_map/ppermute | solution.py:396
  16.8 0.0 collective-permute-done.4
  16.8 1.6 %collective-permute-done.3 = f32[120,128]{1,0:T(8,128)S(1)} collective-permute-done((f32[120,128]{1,0:T(8,128)S(1)}, f32[120,128]{1,0:T(8,128)S(1)}, u32[]{:S(2)}, u32[]{:S(2)}) %collective-permute-start.3) | collective-permute-done | bytes 61472 | tf_op jit(solution)/shard_map/ppermute | solution.py:396
  18.3 1.6 %collective-permute-done.2 = f32[120,128]{1,0:T(8,128)S(1)} collective-permute-done((f32[120,128]{1,0:T(8,128)S(1)}, f32[120,128]{1,0:T(8,128)S(1)}, u32[]{:S(2)}, u32[]{:S(2)}) %collective-permute-start.2) | collective-permute-done | bytes 61472 | tf_op jit(solution)/shard_map/ppermute | solution.py:396
  20.0 0.0 copy-start
  20.0 0.0 copy-start.1
  20.0 0.0 copy-start.2
  20.0 0.0 copy-start.3
  20.1 0.0 copy-start.4
  20.1 0.0 copy-start.5
  20.1 0.0 copy-start.6
  20.1 0.9 %collective-permute-start.7 = (f32[480,128]{1,0:T(8,128)S(1)}, f32[480,128]{1,0:T(8,128)S(1)}, u32[]{:S(2)}, u32[]{:S(2)}) collective-permute-start(f32[480,128]{1,0:T(8,128)S(1)} %pad_maximum_fusion.near_ref), channel_id=1, source_target_pairs={{12,0},{13,1},{14,2},{15,3},{0,4},{1,5},{2,6},{3,7},{4,8},{5,9},{6... | collective-permute-start | bytes 737288 | tf_op jit(solution)/shard_map/ppermute | solution.py:401
  21.0 0.8 %collective-permute-start.6 = (f32[480,128]{1,0:T(8,128)S(1)}, f32[480,128]{1,0:T(8,128)S(1)}, u32[]{:S(2)}, u32[]{:S(2)}) collective-permute-start(f32[480,128]{1,0:T(8,128)S(1)} %pad_maximum_fusion.near_ref), channel_id=1, source_target_pairs={{8,0},{9,1},{10,2},{11,3},{12,4},{13,5},{14,6},{15,7},{0,8},{1,9},... | collective-permute-start | bytes 737288 | tf_op jit(solution)/shard_map/ppermute | solution.py:401
  21.9 0.9 %collective-permute-start.5 = (f32[480,128]{1,0:T(8,128)S(1)}, f32[480,128]{1,0:T(8,128)S(1)}, u32[]{:S(2)}, u32[]{:S(2)}) collective-permute-start(f32[480,128]{1,0:T(8,128)S(1)} %pad_maximum_fusion.near_ref), channel_id=1, source_target_pairs={{4,0},{5,1},{6,2},{7,3},{8,4},{9,5},{10,6},{11,7},{12,8},{13,9},{1... | collective-permute-start | bytes 737288 | tf_op jit(solution)/shard_map/ppermute | solution.py:401
  22.7 4.7 %load.1 = (bf16[2,24,4,128,128]{4,3,2,1,0:T(8,128)(2,1)S(1)}, bf16[2,24,4,128,128]{4,3,2,1,0:T(8,128)(2,1)S(1)}) custom-call(bf16[2,24,4,128,128]{4,3,2,1,0:T(8,128)(2,1)} %explicit_ref, bf16[2,24,4,128,128]{4,3,2,1,0:T(8,128)(2,1)} %implicit_ref), custom_call_target="tpu_custom_call" | custom-call | bytes 25165824 | tf_op jit(solution)/shard_map/load/pallas_call | solution.py:205
  27.4 1.6 %collective-permute-done.7.back_ref = f32[480,128]{1,0:T(8,128)S(1)} collective-permute-done((f32[480,128]{1,0:T(8,128)S(1)}, f32[480,128]{1,0:T(8,128)S(1)}, u32[]{:S(2)}, u32[]{:S(2)}) %collective-permute-start.7) | collective-permute-done | bytes 245792 | tf_op jit(solution)/shard_map/ppermute | solution.py:401
  29.0 0.0 collective-permute-done.6.far_ref
  29.0 2.1 %collective-permute-done.5.next_ref = f32[480,128]{1,0:T(8,128)S(1)} collective-permute-done((f32[480,128]{1,0:T(8,128)S(1)}, f32[480,128]{1,0:T(8,128)S(1)}, u32[]{:S(2)}, u32[]{:S(2)}) %collective-permute-start.5) | collective-permute-done | bytes 245792 | tf_op jit(solution)/shard_map/ppermute | solution.py:401
  31.1 0.0 collective-permute-done.9.right_ref
  31.1 0.0 collective-permute-done.8.left_ref
  31.1 0.0 copy-done
  31.1 0.0 copy-done.1
  31.1 0.0 copy-done.2
  31.1 0.0 copy-done.3
  31.2 0.0 copy-done.4
  31.2 0.0 copy-done.5
  31.2 0.0 copy-done.6
  31.2 5.2 %first.1 = (f32[64,512]{1,0:T(8,128)S(1)}, f32[64,256]{1,0:T(8,128)S(1)}, bf16[24,128,128]{2,1,0:T(8,128)(2,1)S(1)}) custom-call(s32[1]{0:T(128)} %bitcast.origin_ref, s32[4,24]{1,0:T(4,128)S(1)} %bitcast.6, s32[24]{0:T(128)S(1)} %copy-done.4, s32[2]{0:T(128)S(1)} %copy-done.5, s32[2]{0:T(128)S(1)} %copy-done.6, ...), custom_call_target="tpu_custom_call" | custom-call | flops 1711276032 | bytes 8388608 | tf_op jit(solution)/shard_map/first/pallas_call | solution.py:331
  36.4 0.0 collective-permute-start.10
  36.4 2.9 %collective-permute-start.11 = (f32[64,256]{1,0:T(8,128)S(1)}, f32[64,256]{1,0:T(8,128)S(1)}, u32[]{:S(2)}, u32[]{:S(2)}) collective-permute-start(f32[64,256]{1,0:T(8,128)S(1)} %get-tuple-element.37), channel_id=1, source_target_pairs={{16,0},{32,16},{48,32},{64,48},{80,64},{96,80},{112,96},{128,112},... | collective-permute-start | bytes 196616 | tf_op jit(solution)/shard_map/ppermute | solution.py:424
  39.4 2.5 %inner.1.middle_in_ref = bf16[24,128,128]{2,1,0:T(8,128)(2,1)S(1)} custom-call(s32[1]{0:T(128)} %bitcast.origin_ref, s32[4,24]{1,0:T(4,128)S(1)} %bitcast.7, s32[24]{0:T(128)S(1)} %copy-done.4, s32[2]{0:T(128)S(1)} %copy-done.5, s32[2]{0:T(128)S(1)} %copy-done.6, bf16[24,128,128]{2,1,0:T(8,128)(2,1)S(1)} %get-tuple-element.38.field_ref, ...), custom_call_target="tpu_custom_call" | custom-call | flops 704643072 | bytes 8388608 | tf_op jit(solution)/shard_map/inner/pallas_call | solution.py:331
  41.9 0.0 collective-permute-done.11.high_in_ref
  41.9 0.1 collective-permute-done.10.low_in_ref
  42.0 4.0 %last.1 = f32[4,3072]{1,0:T(4,128)} custom-call(s32[1]{0:T(128)} %bitcast.origin_ref, s32[4,24]{1,0:T(4,128)S(1)} %bitcast.8, s32[24]{0:T(128)S(1)} %copy-done.4, s32[2]{0:T(128)S(1)} %copy-done.5, s32[2]{0:T(128)S(1)} %copy-done.6, f32[64,512]{1,0:T(8,128)S(1)} %collective-permute-done.10.low_in_ref, f32[64,256]{1,0:T(8,128)S(1)} %collective-permute-done.11.high_in_ref, ...), custom_call_target="tpu_custom_call" | custom-call | flops 1006632960 | bytes 8388608 | tf_op jit(solution)/shard_map/last/pallas_call | solution.py:331
  (5 shorter events, 0.1 us)
Async XLA Ops:
  0.0 8.0 %collective-permute-start = (f32[4,3072]{1,0:T(4,128)}, f32[4,3072]{1,0:T(4,128)S(1)}, u32[]{:S(2)}, u32[]{:S(2)}) collective-permute-start(f32[4,3072]{1,0:T(4,128)} %param.10), channel_id=1, source_target_pairs={{0,16},{16,32},{32,48},{48,64},{64,80},{80,96},{96,112},{112,128},... | collective-permute-start | bytes 147464 | tf_op jit(solution)/shard_map/ppermute | solution.py:367
  0.0 8.0 %collective-permute-start.1 = (f32[4,3072]{1,0:T(4,128)}, f32[4,3072]{1,0:T(4,128)S(1)}, u32[]{:S(2)}, u32[]{:S(2)}) collective-permute-start(f32[4,3072]{1,0:T(4,128)} %param.10), channel_id=1, source_target_pairs={{16,0},{32,16},{48,32},{64,48},{80,64},{96,80},{112,96},{128,112},... | collective-permute-start | bytes 147464 | tf_op jit(solution)/shard_map/ppermute | solution.py:368
  5.3 5.7 %copy-start.7 = (f32[4,3072]{1,0:T(4,128)S(1)}, f32[4,3072]{1,0:T(4,128)}, u32[]{:S(2)}) copy-start(f32[4,3072]{1,0:T(4,128)} %param.10) | copy-start | bytes 147460
  8.0 23.1 %collective-permute-start.8 = (f32[2,2,4,128,128]{4,3,2,1,0:T(8,128)}, f32[2,2,4,128,128]{4,3,2,1,0:T(8,128)S(1)}, u32[]{:S(2)}, u32[]{:S(2)}) collective-permute-start(f32[2,2,4,128,128]{4,3,2,1,0:T(8,128)} %get-tuple-element.31), channel_id=1, source_target_pairs={{0,16},{16,32},{32,48},{48,64},{64,80},{80,96},{96,112},{112,128},... | collective-permute-start | bytes 3145736 | tf_op jit(solution)/shard_map/ppermute | solution.py:403
  8.0 23.1 %collective-permute-start.9 = (f32[2,1,4,128,128]{4,3,2,1,0:T(8,128)}, f32[2,1,4,128,128]{4,3,2,1,0:T(8,128)S(1)}, u32[]{:S(2)}, u32[]{:S(2)}) collective-permute-start(f32[2,1,4,128,128]{4,3,2,1,0:T(8,128)} %get-tuple-element.32), channel_id=1, source_target_pairs={{16,0},{32,16},{48,32},{64,48},{80,64},{96,80},{112,96},{128,112},... | collective-permute-start | bytes 1572872 | tf_op jit(solution)/shard_map/ppermute | solution.py:404
  11.0 5.7 %collective-permute-start.4 = (f32[120,128]{1,0:T(8,128)S(1)}, f32[120,128]{1,0:T(8,128)S(1)}, u32[]{:S(2)}, u32[]{:S(2)}) collective-permute-start(f32[120,128]{1,0:T(8,128)S(1)} %reshape.11), channel_id=1, source_target_pairs={{3,0},{0,1},{1,2},{2,3},{7,4},{4,5},{5,6},{6,7},{11,8},{8,9},{9,10... | collective-permute-start | bytes 184328 | tf_op jit(solution)/shard_map/ppermute | solution.py:396
  12.6 5.7 %collective-permute-start.3 = (f32[120,128]{1,0:T(8,128)S(1)}, f32[120,128]{1,0:T(8,128)S(1)}, u32[]{:S(2)}, u32[]{:S(2)}) collective-permute-start(f32[120,128]{1,0:T(8,128)S(1)} %reshape.11), channel_id=1, source_target_pairs={{2,0},{3,1},{0,2},{1,3},{6,4},{7,5},{4,6},{5,7},{10,8},{11,9},{8,1... | collective-permute-start | bytes 184328 | tf_op jit(solution)/shard_map/ppermute | solution.py:396
  15.3 4.6 %collective-permute-start.2 = (f32[120,128]{1,0:T(8,128)S(1)}, f32[120,128]{1,0:T(8,128)S(1)}, u32[]{:S(2)}, u32[]{:S(2)}) collective-permute-start(f32[120,128]{1,0:T(8,128)S(1)} %reshape.11), channel_id=1, source_target_pairs={{1,0},{2,1},{3,2},{0,3},{5,4},{6,5},{7,6},{4,7},{9,8},{10,9},{11,1... | collective-permute-start | bytes 184328 | tf_op jit(solution)/shard_map/ppermute | solution.py:396
  20.0 11.1 %copy-start = (bf16[128,128]{1,0:T(8,128)(2,1)S(1)}, bf16[128,128]{1,0:T(8,128)(2,1)}, u32[]{:S(2)}) copy-start(bf16[128,128]{1,0:T(8,128)(2,1)} %get-tuple-element.33.mixing_ref) | copy-start | bytes 98308
  20.0 11.1 %copy-start.1 = (f32[64,128]{1,0:T(8,128)S(1)}, f32[64,128]{1,0:T(8,128)}, u32[]{:S(2)}) copy-start(f32[64,128]{1,0:T(8,128)} %get-tuple-element.34.bias_ref) | copy-start | bytes 98308
  20.0 11.1 %copy-start.2 = (f32[64,128]{1,0:T(8,128)S(1)}, f32[64,128]{1,0:T(8,128)}, u32[]{:S(2)}) copy-start(f32[64,128]{1,0:T(8,128)} %get-tuple-element.35.rate_ref) | copy-start | bytes 98308
  20.0 11.1 %copy-start.3 = (s32[24,4]{0,1:T(4,128)S(1)}, s32[24,4]{0,1:T(4,128)}, u32[]{:S(2)}) copy-start(s32[24,4]{0,1:T(4,128)} %param.13) | copy-start | bytes 1156
  20.1 11.1 %copy-start.4 = (s32[24]{0:T(128)S(1)}, s32[24]{0:T(128)}, u32[]{:S(2)}) copy-start(s32[24]{0:T(128)} %count_ref.7) | copy-start | bytes 292
  20.1 11.1 %copy-start.5 = (s32[2]{0:T(128)S(1)}, s32[2]{0:T(128)}, u32[]{:S(2)}) copy-start(s32[2]{0:T(128)} %month_ref.5) | copy-start | bytes 28
  20.1 11.1 %copy-start.6 = (s32[2]{0:T(128)S(1)}, s32[2]{0:T(128)}, u32[]{:S(2)}) copy-start(s32[2]{0:T(128)} %weight_ref.5) | copy-start | bytes 28
  20.1 8.9 %collective-permute-start.7 = (f32[480,128]{1,0:T(8,128)S(1)}, f32[480,128]{1,0:T(8,128)S(1)}, u32[]{:S(2)}, u32[]{:S(2)}) collective-permute-start(f32[480,128]{1,0:T(8,128)S(1)} %pad_maximum_fusion.near_ref), channel_id=1, source_target_pairs={{12,0},{13,1},{14,2},{15,3},{0,4},{1,5},{2,6},{3,7},{4,8},{5,9},{6... | collective-permute-start | bytes 737288 | tf_op jit(solution)/shard_map/ppermute | solution.py:401
  21.0 8.0 %collective-permute-start.6 = (f32[480,128]{1,0:T(8,128)S(1)}, f32[480,128]{1,0:T(8,128)S(1)}, u32[]{:S(2)}, u32[]{:S(2)}) collective-permute-start(f32[480,128]{1,0:T(8,128)S(1)} %pad_maximum_fusion.near_ref), channel_id=1, source_target_pairs={{8,0},{9,1},{10,2},{11,3},{12,4},{13,5},{14,6},{15,7},{0,8},{1,9},... | collective-permute-start | bytes 737288 | tf_op jit(solution)/shard_map/ppermute | solution.py:401
  21.9 9.2 %collective-permute-start.5 = (f32[480,128]{1,0:T(8,128)S(1)}, f32[480,128]{1,0:T(8,128)S(1)}, u32[]{:S(2)}, u32[]{:S(2)}) collective-permute-start(f32[480,128]{1,0:T(8,128)S(1)} %pad_maximum_fusion.near_ref), channel_id=1, source_target_pairs={{4,0},{5,1},{6,2},{7,3},{8,4},{9,5},{10,6},{11,7},{12,8},{13,9},{1... | collective-permute-start | bytes 737288 | tf_op jit(solution)/shard_map/ppermute | solution.py:401
  36.4 5.6 %collective-permute-start.10 = (f32[64,512]{1,0:T(8,128)S(1)}, f32[64,512]{1,0:T(8,128)S(1)}, u32[]{:S(2)}, u32[]{:S(2)}) collective-permute-start(f32[64,512]{1,0:T(8,128)S(1)} %get-tuple-element.36), channel_id=1, source_target_pairs={{0,16},{16,32},{32,48},{48,64},{64,80},{80,96},{96,112},{112,128},... | collective-permute-start | bytes 393224 | tf_op jit(solution)/shard_map/ppermute | solution.py:423
  36.4 5.4 %collective-permute-start.11 = (f32[64,256]{1,0:T(8,128)S(1)}, f32[64,256]{1,0:T(8,128)S(1)}, u32[]{:S(2)}, u32[]{:S(2)}) collective-permute-start(f32[64,256]{1,0:T(8,128)S(1)} %get-tuple-element.37), channel_id=1, source_target_pairs={{16,0},{32,16},{48,32},{64,48},{80,64},{96,80},{112,96},{128,112},... | collective-permute-start | bytes 196616 | tf_op jit(solution)/shard_map/ppermute | solution.py:424

commit v4 on v3

--- a/solution.py
+++ b/solution.py
@@ -16,6 +16,7 @@
 BF16 = jnp.bfloat16
 MIB = 1 << 20
 SIDE = 4
+TILE = 16
 NT = (((1,), (1,)), ((), ()))
 
 
@@ -35,11 +36,16 @@
     )
 
 
-def combine(product, coef):
+def own_store(ref, where, value):
+    high = value.astype(BF16).astype(F32)
+    spare = jnp.zeros((TILE - 2 * value.shape[0], value.shape[1]), F32)
+    ref[where] = jnp.concatenate([high, value - high, spare], axis=0).astype(BF16)
+
+
+def combine(product, coef, half):
     block = product.shape[1] // 2
-    half = product.shape[0] // 2
     mixed = coef[0] * product[:, :block] + coef[1] * product[:, block:]
-    return mixed[:half] + mixed[half:]
+    return mixed[:half] + mixed[half : 2 * half]
 
 
 def column(total, origin_ref, cols_ref, count_ref, row, r, spare):
@@ -49,7 +55,7 @@
     return jnp.where(r < count_ref[row], at, spare)
 
 
-def own_row(values_ref, blocks_ref, tables, row, shift, coef):
+def own_row(values_ref, blocks_ref, tables, row, shift, coef, half):
     width = blocks_ref.shape[2]
     spare = blocks_ref.shape[1] + LOW + HIGH
     left = jnp.concatenate(
@@ -63,10 +69,10 @@
         axis=0,
     )
     product = lax.dot_general(left, right, NT, preferred_element_type=F32)
-    return combine(product, coef)
-
-
-def edge_row(values_ref, edge_ref, row, first, coef):
+    return combine(product, coef, half)
+
+
+def edge_row(values_ref, edge_ref, row, first, coef, half):
     width = edge_ref.shape[2]
     left = jnp.concatenate([values_ref[first + d] for d in range(width)], axis=1)
     right = jnp.concatenate(
@@ -77,18 +83,18 @@
         axis=0,
     )
     product = lax.dot_general(left, right, NT, preferred_element_type=F32)
-    return combine(product, coef)
-
-
-def prepare_source(side, part, place, mix_ref, bias_ref, rate_ref, mixing_ref, bias_out_ref, rate_out_ref):
+    return combine(product, coef, half)
+
+
+def prepare_source(side, part, place, mix_ref, bias_ref, rate_ref, mixing_ref, own_ref, bias_out_ref, rate_out_ref):
     size = mix_ref.shape[0]
     mine = size // (side * side)
     at = lax.broadcasted_iota(jnp.int32, (size, size), 0)
     wanted = lax.broadcasted_iota(jnp.int32, (size, size), 1)
     outer, inner = at // (mine * side), lax.rem(at // mine, side)
     even = lax.rem(part, 2) == 0
-    y = lax.rem(place // side + jnp.where(even, outer, inner), side)
-    x = lax.rem(lax.rem(place, side) + jnp.where(even, inner, outer), side)
+    y = lax.rem(place // side + side - jnp.where(even, outer, inner), side)
+    x = lax.rem(lax.rem(place, side) + side - jnp.where(even, inner, outer), side)
     chosen = (y * side + x) * mine + lax.rem(at, mine) == wanted
     pick = jnp.where(chosen, 1.0, 0.0).astype(BF16)
     mix = mix_ref[...]
@@ -99,9 +105,12 @@
         rows = lax.dot_general(
             pick, piece, (((1,), (0,)), ((), ())), preferred_element_type=F32
         ).astype(BF16)
-        tiles.append(lax.dot_general(rows, pick, NT, preferred_element_type=F32).astype(BF16))
-    tile = jnp.concatenate(tiles, axis=0)
+        tiles.append(lax.dot_general(rows, pick, NT, preferred_element_type=F32))
+    tile = jnp.concatenate(tiles, axis=0).astype(BF16)
     mixing_ref[...] = jnp.concatenate([tile, tile], axis=1)
+    spare = jnp.zeros((TILE - 2 * mine, size), F32)
+    tile = jnp.concatenate([tiles[0][:mine], tiles[1][:mine], spare], axis=0).astype(BF16)
+    own_ref[...] = jnp.concatenate([tile, tile], axis=1)
     for source_ref, target_ref, scale in ((bias_ref, bias_out_ref, 1.0), (rate_ref, rate_out_ref, 0.5)):
         column = jnp.sum(jnp.where(chosen, source_ref[...], 0.0), axis=1, keepdims=True)
         target_ref[...] = jnp.broadcast_to(scale * column, target_ref.shape)
@@ -119,15 +128,15 @@
     both = lax.dot_general(
         mixing, values, (((1,), (0,)), ((), ())), preferred_element_type=F32
     )
-    half = both.shape[0] // 2
-    inner = both[:half] + both[half:] + bias
+    half = bias.shape[0]
+    inner = both[:half] + both[half : 2 * half] + bias
     return rate * inner * jnp.exp(-0.125 * inner * inner)
 
 
 def edges_kernel(
     total, side, origin_ref, place_ref, cols_ref, count_ref, low_ref, high_ref,
     mix_ref, bias_ref, rate_ref,
-    to_right_ref, to_left_ref, mixing_ref, bias_out_ref, rate_out_ref,
+    to_right_ref, to_left_ref, mixing_ref, own_ref, bias_out_ref, rate_out_ref,
 ):
     width, rows = cols_ref.shape
     for source_ref, target_ref, start in (
@@ -149,7 +158,8 @@
                 for m in range(2):
                     target_ref[m, row, d] = source_ref[m, row, slot].astype(F32) * scale
     prepare_source(
-        side, origin_ref[0], place_ref[0], mix_ref, bias_ref, rate_ref, mixing_ref, bias_out_ref, rate_out_ref
+        side, origin_ref[0], place_ref[0], mix_ref, bias_ref, rate_ref,
+        mixing_ref, own_ref, bias_out_ref, rate_out_ref,
     )
 
 
@@ -168,11 +178,12 @@
         in_specs=[smem] * 4
         + [spec(REACH, rows // REACH - 1), spec(REACH - 1, 0)]
         + [vmem] * 3,
-        out_specs=[spec(REACH, 0), spec(REACH - 1, 0)] + [vmem] * 3,
+        out_specs=[spec(REACH, 0), spec(REACH - 1, 0)] + [vmem] * 4,
         out_shape=[
             shape(REACH),
             shape(REACH - 1),
             jax.ShapeDtypeStruct((2 * size, 2 * size), BF16),
+            jax.ShapeDtypeStruct((TILE, 2 * size), BF16),
             jax.ShapeDtypeStruct((size, block), F32),
             jax.ShapeDtypeStruct((size, block), F32),
         ],
@@ -220,7 +231,7 @@
 def first_kernel(
     total, origin_ref, cols_ref, count_ref, month_ref, weight_ref, explicit_ref, implicit_ref,
     near_ref, next_ref, far_ref, back_ref, left_ref, right_ref, mixing_ref, bias_ref, rate_ref,
-    low_ref, high_ref, field_out_ref, values_ref, middle_ref,
+    low_ref, high_ref, middle_ref, values_ref,
 ):
     coef = coefficients(month_ref, weight_ref, 0)
     tables = (total, origin_ref, cols_ref, count_ref)
@@ -244,84 +255,96 @@
         split_store(middle_ref, frame, product + source)
 
     for row in range(REACH):
-        finish(row, edge_row(values_ref, left_ref, row, row, coef))
+        finish(row, edge_row(values_ref, left_ref, row, row, coef, tracers))
     for row in range(REACH - 1):
         frame = rows + REACH + row
-        finish(frame, edge_row(values_ref, right_ref, row, frame, coef))
+        finish(frame, edge_row(values_ref, right_ref, row, frame, coef, tracers))
     for row in range(rows):
-        finish(row + REACH, own_row(values_ref, explicit_ref, tables, row, 0, coef))
-
-    for row in [*range(rows - LOW, rows), *range(rows - LOW)]:
-        result = own_row(middle_ref, implicit_ref, tables, row, REACH, coef)
-        split_store(field_out_ref, row, result)
-        if row >= rows - LOW:
-            at = row - (rows - LOW)
-            low_ref[:, at * block : (at + 1) * block] = result
-        if row < HIGH:
-            high_ref[:, row * block : (row + 1) * block] = result
+        finish(row + REACH, own_row(values_ref, explicit_ref, tables, row, 0, coef, tracers))
+    for at in range(LOW):
+        low_ref[:, at * block : (at + 1) * block] = own_row(
+            middle_ref, implicit_ref, tables, rows - LOW + at, REACH, coef, tracers
+        )
+    for row in range(HIGH):
+        high_ref[:, row * block : (row + 1) * block] = own_row(
+            middle_ref, implicit_ref, tables, row, REACH, coef, tracers
+        )
 
 
 def inner_kernel(
-    total, origin_ref, cols_ref, count_ref, month_ref, weight_ref, field_ref, explicit_ref, mixing_ref, bias_ref, rate_ref,
-    middle_ref, values_ref,
+    total, origin_ref, cols_ref, count_ref, month_ref, weight_ref, explicit_ref, implicit_ref,
+    low_ref, high_ref, middle_ref, mixing_ref, bias_ref, rate_ref,
+    field_ref, own_ref, own_middle_ref,
 ):
-    coef = coefficients(month_ref, weight_ref, 1)
+    coef = coefficients(month_ref, weight_ref, 0)
     tables = (total, origin_ref, cols_ref, count_ref)
     rows = explicit_ref.shape[1]
-    values_ref[LOW : LOW + rows] = field_ref[...]
-    values_ref[rows + LOW + HIGH] = jnp.zeros(values_ref.shape[1:], BF16)
-    mixing, bias, rate = mixing_ref[...], bias_ref[...], rate_ref[...]
-
-    def explicit_row(row, carry):
-        product = own_row(values_ref, explicit_ref, tables, row, 0, coef)
-        source = half_source(values_ref[row + LOW], mixing, bias, rate)
-        split_store(middle_ref, row, product + source)
-        return carry
-
+    block = explicit_ref.shape[-1]
+    tracers = low_ref.shape[0]
+    mine = bias_ref.shape[0] // (SIDE * SIDE)
+    ext = rows + LOW + HIGH
+
+    def put(row, result):
+        split_store(field_ref, row, result)
+        own_store(own_ref, row + LOW, result[:mine])
+
+    for at in range(LOW):
+        put(rows - LOW + at, low_ref[:, at * block : (at + 1) * block])
+    for row in range(HIGH):
+        put(row, high_ref[:, row * block : (row + 1) * block])
+    for row in range(HIGH, rows - LOW):
+        put(row, own_row(middle_ref, implicit_ref, tables, row, REACH, coef, tracers))
+    own_ref[ext] = jnp.zeros((TILE, block), BF16)
+    coef = coefficients(month_ref, weight_ref, 1)
+    mixing, bias, rate = mixing_ref[...], bias_ref[:mine, :], rate_ref[:mine, :]
     for row in range(REACH, rows - REACH + 1):
-        explicit_row(row, 0)
+        product = own_row(own_ref, explicit_ref, tables, row, 0, coef, mine)
+        source = half_source(field_ref[row], mixing, bias, rate)
+        own_store(own_middle_ref, row + REACH, product + source)
 
 
 def last_kernel(
-    total, origin_ref, cols_ref, count_ref, month_ref, weight_ref, low_in_ref, high_in_ref, field_ref, middle_in_ref,
-    explicit_ref, implicit_ref, left_ref, right_ref, mixing_ref, bias_ref, rate_ref,
-    out_ref, values_ref, middle_ref, result_ref,
+    total, origin_ref, cols_ref, count_ref, month_ref, weight_ref, low_in_ref, high_in_ref,
+    field_ref, own_in_ref, own_middle_in_ref, explicit_ref, implicit_ref, left_ref, right_ref,
+    mixing_ref, bias_ref, rate_ref, out_ref, halo_ref, own_ref, own_middle_ref,
 ):
     coef = coefficients(month_ref, weight_ref, 1)
     tables = (total, origin_ref, cols_ref, count_ref)
     rows = explicit_ref.shape[1]
     block = explicit_ref.shape[-1]
-    tracers = bias_ref.shape[0]
+    mine = bias_ref.shape[0] // (SIDE * SIDE)
     ext = rows + LOW + HIGH
-    zero = jnp.zeros((2 * tracers, block), BF16)
-    values_ref[ext] = zero
-    middle_ref[ext - REACH] = zero
-    values_ref[LOW : LOW + rows] = field_ref[...]
-    middle_ref[2 * REACH : rows + 1] = middle_in_ref[REACH : rows - REACH + 1]
-    for b in range(LOW):
-        split_store(values_ref, b, exchanged(low_in_ref[:, b * block : (b + 1) * block]))
-    for b in range(HIGH):
-        value = exchanged(high_in_ref[:, b * block : (b + 1) * block])
-        split_store(values_ref, LOW + rows + b, value)
-    mixing, bias, rate = mixing_ref[...], bias_ref[...], rate_ref[...]
-
-    def finish(frame, product):
-        source = half_source(values_ref[frame + REACH], mixing, bias, rate)
-        split_store(middle_ref, frame, product + source)
+    own_ref[LOW : LOW + rows] = own_in_ref[LOW : LOW + rows]
+    own_ref[ext] = jnp.zeros((TILE, block), BF16)
+    own_middle_ref[2 * REACH : rows + 1] = own_middle_in_ref[2 * REACH : rows + 1]
+    own_middle_ref[ext - REACH] = jnp.zeros((TILE, block), BF16)
+    for b in range(LOW + HIGH):
+        if b < LOW:
+            value, frame = low_in_ref[:, b * block : (b + 1) * block], b
+        else:
+            value, frame = high_in_ref[:, (b - LOW) * block : (b - LOW + 1) * block], rows + b
+        value = exchanged(value)
+        split_store(halo_ref, b, value)
+        own_store(own_ref, frame, value[:mine])
+    mixing, bias, rate = mixing_ref[...], bias_ref[:mine, :], rate_ref[:mine, :]
+
+    def finish(frame, values, product):
+        own_store(own_middle_ref, frame, product + half_source(values, mixing, bias, rate))
 
     for row in range(REACH):
-        finish(row, edge_row(values_ref, left_ref, row, row, coef))
+        product = edge_row(own_ref, left_ref, row, row, coef, mine)
+        finish(row, halo_ref[row + REACH], product)
     for row in range(REACH - 1):
         frame = rows + REACH + row
-        finish(frame, edge_row(values_ref, right_ref, row, frame, coef))
+        product = edge_row(own_ref, right_ref, row, frame, coef, mine)
+        finish(frame, halo_ref[LOW + row], product)
     for row in [*range(REACH), *range(rows - REACH + 1, rows)]:
-        finish(row + REACH, own_row(values_ref, explicit_ref, tables, row, 0, coef))
-
+        product = own_row(own_ref, explicit_ref, tables, row, 0, coef, mine)
+        finish(row + REACH, field_ref[row], product)
     for row in range(rows):
-        result_ref[:, row * block : (row + 1) * block] = own_row(
-            middle_ref, implicit_ref, tables, row, REACH, coef
+        out_ref[:, row * block : (row + 1) * block] = own_row(
+            own_middle_ref, implicit_ref, tables, row, REACH, coef, mine
         )
-    out_ref[...] = result_ref[: out_ref.shape[0], :]
 
 
 def call(kernel, name, smem_count, hbm_count, args, outs, scratch, flops, limit):
@@ -386,9 +409,9 @@
             for t in range(groups):
                 y, x = divmod(t, SIDE)
                 if (p + stage) % 2 == 0:
-                    source_at = y * SIDE + (x + k) % SIDE
+                    source_at = y * SIDE + (x - k) % SIDE
                 else:
-                    source_at = (y + k) % SIDE * SIDE + x
+                    source_at = (y - k) % SIDE * SIDE + x
                 moves.append((p * groups + source_at, p * groups + t))
         return moves
 
@@ -406,37 +429,44 @@
     shape = jax.ShapeDtypeStruct
     stack = lambda count: pltpu.VMEM((count, 2 * total, block), BF16)
     one = 2 * 2 * total * 2 * block * width * block
-    low, high, field = call(
+    own = lambda count: shape((count, TILE, block), BF16)
+    mixing, own_mixing, bias, rate = source
+    own_source = (own_mixing, bias, rate)
+    low, high, middle = call(
         functools.partial(first_kernel, rows * parts), "first", 5, 0,
-        (*scalars, explicit_blocks, implicit_blocks, *gathered, left, right, *source),
+        (
+            *scalars, explicit_blocks, implicit_blocks, *gathered, left, right,
+            mixing, bias, rate,
+        ),
         [
             shape((total, LOW * block), F32),
             shape((total, HIGH * block), F32),
-            shape((rows, 2 * total, block), BF16),
-        ],
-        [
-            stack(ext + 1),
-            stack(ext - REACH + 1),
-        ],
-        51 * one, 12,
-    )
-    low = lax.ppermute(low, "pts", forward)
-    high = lax.ppermute(high, "pts", backward)
-    (middle,) = call(
+            shape((ext - REACH + 1, 2 * total, block), BF16),
+        ],
+        [stack(ext + 1)],
+        33 * one, 12,
+    )
+    low_in = lax.ppermute(low, "pts", forward)
+    high_in = lax.ppermute(high, "pts", backward)
+    field, own_field, own_middle = call(
         functools.partial(inner_kernel, rows * parts), "inner", 5, 0,
-        (*scalars, field, explicit_blocks, *source),
-        [shape((rows, 2 * total, block), BF16)],
-        [stack(ext + 1)],
-        21 * one, 12,
+        (*scalars, explicit_blocks, implicit_blocks, low, high, middle, *own_source),
+        [shape((rows, 2 * total, block), BF16), own(ext + 1), own(ext - REACH + 1)],
+        [],
+        39 * one, 12,
     )
     (advanced,) = call(
         functools.partial(last_kernel, rows * parts), "last", 5, 0,
         (
-            *scalars, low, high, field, middle, explicit_blocks, implicit_blocks,
-            left, right, *source,
+            *scalars, low_in, high_in, field, own_field, own_middle,
+            explicit_blocks, implicit_blocks, left, right, *own_source,
         ),
         [shape((mine, rows * block), F32)],
-        [stack(ext + 1), stack(ext - REACH + 1), pltpu.VMEM((total, rows * block), F32)],
+        [
+            stack(LOW + HIGH),
+            pltpu.VMEM((ext + 1, TILE, block), BF16),
+            pltpu.VMEM((ext - REACH + 1, TILE, block), BF16),
+        ],
         30 * one, 12,
     )
     return advanced

time: 46.5 us -> 45.5 us (0.978)
  Pallas kernels: 19.1 us -> 18.6 us
    pallas_call x3, Pallas kernels: 11.7 us -> 11.2 us  [call(): pl.pallas_call(kernel, in_specs=[smem] * smem_count + [hbm] * hbm_count +...]
  transfers between devices with their start and end apart: 12 -> 12, of which waited for: 5 -> 4; matrix products, arithmetic and copies ran while one was open for 0% -> 0% of each run, Pallas kernels for 21% -> 25%
where the time goes in v4:
time: 45.5 us; the launch traced here: 45.4 us
  starting transfers between devices  19.6 us (43%)
  Pallas kernels  18.6 us (41%)
  waiting for transfers between devices  6.92 us (15%)
    pallas_call x3, Pallas kernels, call(): pl.pallas_call(kernel, in_specs=[smem] * smem_count + [hbm] * hbm_count +...  11.2 us
    ppermute x3, starting transfers between devices, per_device(): lax.ppermute(extended, both, along(0, k))  5.73 us
    ppermute x1, starting transfers between devices, per_device(): high = lax.ppermute(tracers, 'pts', backward)[:, :HIGH * block]  5.3 us
    pallas_call x1, Pallas kernels, load(): pl.pallas_call(load_kernel, in_specs=[hbm, hbm], out_specs=[vmem, vmem],...  4.7 us
    ppermute x3, waiting for transfers between devices, per_device(): lax.ppermute(line, both, along(1, k))  3.69 us
    ppermute x3, waiting for transfers between devices, per_device(): lax.ppermute(extended, both, along(0, k))  3.21 us
    ppermute x1, starting transfers between devices, per_device(): right = lax.ppermute(to_left, 'pts', backward)  2.94 us
    ppermute x1, starting transfers between devices, per_device(): high_in = lax.ppermute(high, 'pts', backward)  2.94 us
  transfers between devices with their start and end apart: 12, of which 4 were waited for; matrix products, arithmetic and copies ran while one was open for 0% of the time, Pallas kernels for 25%

profile of v4, /device:TPU:16, one launch (start us, length us, event | category | flops | bytes accessed | tf_op | source)
XLA Modules:
  0.0 45.4 jit_solution(1159087149219600252)
XLA Ops:
  0.0 0.0 collective-permute-start
  0.0 5.3 %collective-permute-start.1 = (f32[4,3072]{1,0:T(4,128)}, f32[4,3072]{1,0:T(4,128)S(1)}, u32[]{:S(2)}, u32[]{:S(2)}) collective-permute-start(f32[4,3072]{1,0:T(4,128)} %param.10), channel_id=1, source_target_pairs={{16,0},{32,16},{48,32},{64,48},{80,64},{96,80},{112,96},{128,112},... | collective-permute-start | bytes 147464 | tf_op jit(solution)/shard_map/ppermute | solution.py:391
  5.3 0.0 copy-start.8
  5.3 2.7 %edges.1 = (f32[2,2,4,128,128]{4,3,2,1,0:T(8,128)}, f32[2,1,4,128,128]{4,3,2,1,0:T(8,128)}, bf16[128,128]{1,0:T(8,128)(2,1)}, bf16[16,128]{1,0:T(8,128)(2,1)}, f32[64,128]{1,0:T(8,128)}, /*index=5*/f32[64,128]{1,0:T(8,128)}) custom-call(s32[1]{0:T(128)} %bitcast.origin_ref, s32[1]{0:T(128)} %bitcast.2.place_ref, s32[4,24]{1,0:T(4,128)} %bitcast.5, ...), custom_call_target="tpu_custom_call" | custom-call | tf_op jit(solution)/shard_map/edges/pallas_call | solution.py:175
  8.0 0.0 collective-permute-done
  8.0 0.0 collective-permute-done.1
  8.0 0.0 collective-permute-start.8
  8.1 2.9 %collective-permute-start.9 = (f32[2,1,4,128,128]{4,3,2,1,0:T(8,128)}, f32[2,1,4,128,128]{4,3,2,1,0:T(8,128)S(1)}, u32[]{:S(2)}, u32[]{:S(2)}) collective-permute-start(f32[2,1,4,128,128]{4,3,2,1,0:T(8,128)} %get-tuple-element.36), channel_id=1, source_target_pairs={{16,0},{32,16},{48,32},{64,48},{80,64},{96,80},{112,96},{128,112},... | collective-permute-start | bytes 1572872 | tf_op jit(solution)/shard_map/ppermute | solution.py:427
  11.0 0.0 copy-done.8
  11.1 1.6 %collective-permute-start.2 = (f32[120,128]{1,0:T(8,128)S(1)}, f32[120,128]{1,0:T(8,128)S(1)}, u32[]{:S(2)}, u32[]{:S(2)}) collective-permute-start(f32[120,128]{1,0:T(8,128)S(1)} %reshape.11), channel_id=1, source_target_pairs={{3,0},{0,1},{1,2},{2,3},{7,4},{4,5},{5,6},{6,7},{11,8},{8,9},{9,10... | collective-permute-start | bytes 184328 | tf_op jit(solution)/shard_map/ppermute | solution.py:419
  12.6 2.7 %collective-permute-start.3 = (f32[120,128]{1,0:T(8,128)S(1)}, f32[120,128]{1,0:T(8,128)S(1)}, u32[]{:S(2)}, u32[]{:S(2)}) collective-permute-start(f32[120,128]{1,0:T(8,128)S(1)} %reshape.11), channel_id=1, source_target_pairs={{2,0},{3,1},{0,2},{1,3},{6,4},{7,5},{4,6},{5,7},{10,8},{11,9},{8,1... | collective-permute-start | bytes 184328 | tf_op jit(solution)/shard_map/ppermute | solution.py:419
  15.4 1.4 %collective-permute-start.4 = (f32[120,128]{1,0:T(8,128)S(1)}, f32[120,128]{1,0:T(8,128)S(1)}, u32[]{:S(2)}, u32[]{:S(2)}) collective-permute-start(f32[120,128]{1,0:T(8,128)S(1)} %reshape.11), channel_id=1, source_target_pairs={{1,0},{2,1},{3,2},{0,3},{5,4},{6,5},{7,6},{4,7},{9,8},{10,9},{11,1... | collective-permute-start | bytes 184328 | tf_op jit(solution)/shard_map/ppermute | solution.py:419
  16.8 0.0 collective-permute-done.2
  16.8 1.6 %collective-permute-done.3 = f32[120,128]{1,0:T(8,128)S(1)} collective-permute-done((f32[120,128]{1,0:T(8,128)S(1)}, f32[120,128]{1,0:T(8,128)S(1)}, u32[]{:S(2)}, u32[]{:S(2)}) %collective-permute-start.3) | collective-permute-done | bytes 61472 | tf_op jit(solution)/shard_map/ppermute | solution.py:419
  18.4 1.6 %collective-permute-done.4 = f32[120,128]{1,0:T(8,128)S(1)} collective-permute-done((f32[120,128]{1,0:T(8,128)S(1)}, f32[120,128]{1,0:T(8,128)S(1)}, u32[]{:S(2)}, u32[]{:S(2)}) %collective-permute-start.4) | collective-permute-done | bytes 61472 | tf_op jit(solution)/shard_map/ppermute | solution.py:419
  20.0 0.0 copy-start
  20.0 0.0 copy-start.1
  20.0 0.0 copy-start.2
  20.1 0.0 copy-start.3
  20.1 0.0 copy-start.5
  20.1 0.0 copy-start.6
  20.1 0.0 copy-start.7
  20.1 0.9 %collective-permute-start.5 = (f32[480,128]{1,0:T(8,128)S(1)}, f32[480,128]{1,0:T(8,128)S(1)}, u32[]{:S(2)}, u32[]{:S(2)}) collective-permute-start(f32[480,128]{1,0:T(8,128)S(1)} %pad_maximum_fusion.near_ref), channel_id=1, source_target_pairs={{12,0},{13,1},{14,2},{15,3},{0,4},{1,5},{2,6},{3,7},{4,8},{5,9},{6... | collective-permute-start | bytes 737288 | tf_op jit(solution)/shard_map/ppermute | solution.py:424
  21.0 0.8 %collective-permute-start.6 = (f32[480,128]{1,0:T(8,128)S(1)}, f32[480,128]{1,0:T(8,128)S(1)}, u32[]{:S(2)}, u32[]{:S(2)}) collective-permute-start(f32[480,128]{1,0:T(8,128)S(1)} %pad_maximum_fusion.near_ref), channel_id=1, source_target_pairs={{8,0},{9,1},{10,2},{11,3},{12,4},{13,5},{14,6},{15,7},{0,8},{1,9},... | collective-permute-start | bytes 737288 | tf_op jit(solution)/shard_map/ppermute | solution.py:424
  21.9 0.9 %collective-permute-start.7 = (f32[480,128]{1,0:T(8,128)S(1)}, f32[480,128]{1,0:T(8,128)S(1)}, u32[]{:S(2)}, u32[]{:S(2)}) collective-permute-start(f32[480,128]{1,0:T(8,128)S(1)} %pad_maximum_fusion.near_ref), channel_id=1, source_target_pairs={{4,0},{5,1},{6,2},{7,3},{8,4},{9,5},{10,6},{11,7},{12,8},{13,9},{1... | collective-permute-start | bytes 737288 | tf_op jit(solution)/shard_map/ppermute | solution.py:424
  22.7 4.7 %load.1 = (bf16[2,24,4,128,128]{4,3,2,1,0:T(8,128)(2,1)S(1)}, bf16[2,24,4,128,128]{4,3,2,1,0:T(8,128)(2,1)S(1)}) custom-call(bf16[2,24,4,128,128]{4,3,2,1,0:T(8,128)(2,1)} %explicit_ref, bf16[2,24,4,128,128]{4,3,2,1,0:T(8,128)(2,1)} %implicit_ref), custom_call_target="tpu_custom_call" | custom-call | bytes 25165824 | tf_op jit(solution)/shard_map/load/pallas_call | solution.py:216
  27.4 1.6 %collective-permute-done.5.next_ref = f32[480,128]{1,0:T(8,128)S(1)} collective-permute-done((f32[480,128]{1,0:T(8,128)S(1)}, f32[480,128]{1,0:T(8,128)S(1)}, u32[]{:S(2)}, u32[]{:S(2)}) %collective-permute-start.5) | collective-permute-done | bytes 245792 | tf_op jit(solution)/shard_map/ppermute | solution.py:424
  29.0 0.0 collective-permute-done.6.far_ref
  29.0 2.1 %collective-permute-done.7.back_ref = f32[480,128]{1,0:T(8,128)S(1)} collective-permute-done((f32[480,128]{1,0:T(8,128)S(1)}, f32[480,128]{1,0:T(8,128)S(1)}, u32[]{:S(2)}, u32[]{:S(2)}) %collective-permute-start.7) | collective-permute-done | bytes 245792 | tf_op jit(solution)/shard_map/ppermute | solution.py:424
  31.1 0.0 collective-permute-done.9.right_ref
  31.1 0.0 collective-permute-done.8.left_ref
  31.1 0.0 copy-done
  31.1 0.0 copy-done.1
  31.1 0.0 copy-done.2
  31.2 0.0 copy-done.3
  31.2 0.0 copy-done.5
  31.2 0.0 copy-done.6
  31.2 0.0 copy-done.7
  31.2 0.0 copy-start.4
  31.2 3.7 %first.1 = (f32[64,512]{1,0:T(8,128)S(1)}, f32[64,256]{1,0:T(8,128)S(1)}, bf16[29,128,128]{2,1,0:T(8,128)(2,1)S(1)}) custom-call(s32[1]{0:T(128)} %bitcast.origin_ref, s32[4,24]{1,0:T(4,128)S(1)} %bitcast.6, s32[24]{0:T(128)S(1)} %copy-done.5, s32[2]{0:T(128)S(1)} %copy-done.6, s32[2]{0:T(128)S(1)} %copy-done.7, ...), custom_call_target="tpu_custom_call" | custom-call | flops 1107296256 | bytes 8388608 | tf_op jit(solution)/shard_map/first/pallas_call | solution.py:354
  34.9 0.0 collective-permute-start.10
  34.9 2.9 %collective-permute-start.11 = (f32[64,256]{1,0:T(8,128)S(1)}, f32[64,256]{1,0:T(8,128)S(1)}, u32[]{:S(2)}, u32[]{:S(2)}) collective-permute-start(f32[64,256]{1,0:T(8,128)S(1)} %get-tuple-element.41.high_ref), channel_id=1, source_target_pairs={{16,0},{32,16},{48,32},{64,48},{80,64},{96,80},{112,96},{128,112},... | collective-permute-start | bytes 196616 | tf_op jit(solution)/shard_map/ppermute | solution.py:450
  37.9 0.0 copy-done.4
  37.9 3.9 %inner.1 = (bf16[24,128,128]{2,1,0:T(8,128)(2,1)S(1)}, bf16[31,16,128]{2,1,0:T(8,128)(2,1)S(1)}, bf16[29,16,128]{2,1,0:T(8,128)(2,1)S(1)}) custom-call(s32[1]{0:T(128)} %bitcast.origin_ref, s32[4,24]{1,0:T(4,128)S(1)} %bitcast.7, s32[24]{0:T(128)S(1)} %copy-done.5, s32[2]{0:T(128)S(1)} %copy-done.6, s32[2]{0:T(128)S(1)} %copy-done.7, ...), custom_call_target="tpu_custom_call" | custom-call | flops 1308622848 | bytes 8388608 | tf_op jit(solution)/shard_map/inner/pallas_call | solution.py:354
  41.8 0.0 collective-permute-done.11.high_in_ref
  41.9 0.0 collective-permute-done.10.low_in_ref
  41.9 3.5 %last.1 = f32[4,3072]{1,0:T(4,128)} custom-call(s32[1]{0:T(128)} %bitcast.origin_ref, s32[4,24]{1,0:T(4,128)S(1)} %bitcast.8, s32[24]{0:T(128)S(1)} %copy-done.5, s32[2]{0:T(128)S(1)} %copy-done.6, s32[2]{0:T(128)S(1)} %copy-done.7, f32[64,512]{1,0:T(8,128)S(1)} %collective-permute-done.10.low_in_ref, f32[64,256]{1,0:T(8,128)S(1)} %collective-permute-done.11.high_in_ref, ...), custom_call_target="tpu_custom_call" | custom-call | flops 1006632960 | bytes 8388608 | tf_op jit(solution)/shard_map/last/pallas_call | solution.py:354
  (5 shorter events, 0.1 us)
Async XLA Ops:
  0.0 8.0 %collective-permute-start = (f32[4,3072]{1,0:T(4,128)}, f32[4,3072]{1,0:T(4,128)S(1)}, u32[]{:S(2)}, u32[]{:S(2)}) collective-permute-start(f32[4,3072]{1,0:T(4,128)} %param.10), channel_id=1, source_target_pairs={{0,16},{16,32},{32,48},{48,64},{64,80},{80,96},{96,112},{112,128},... | collective-permute-start | bytes 147464 | tf_op jit(solution)/shard_map/ppermute | solution.py:390
  0.0 8.0 %collective-permute-start.1 = (f32[4,3072]{1,0:T(4,128)}, f32[4,3072]{1,0:T(4,128)S(1)}, u32[]{:S(2)}, u32[]{:S(2)}) collective-permute-start(f32[4,3072]{1,0:T(4,128)} %param.10), channel_id=1, source_target_pairs={{16,0},{32,16},{48,32},{64,48},{80,64},{96,80},{112,96},{128,112},... | collective-permute-start | bytes 147464 | tf_op jit(solution)/shard_map/ppermute | solution.py:391
  5.3 5.7 %copy-start.8 = (f32[4,3072]{1,0:T(4,128)S(1)}, f32[4,3072]{1,0:T(4,128)}, u32[]{:S(2)}) copy-start(f32[4,3072]{1,0:T(4,128)} %param.10) | copy-start | bytes 147460
  8.0 23.1 %collective-permute-start.8 = (f32[2,2,4,128,128]{4,3,2,1,0:T(8,128)}, f32[2,2,4,128,128]{4,3,2,1,0:T(8,128)S(1)}, u32[]{:S(2)}, u32[]{:S(2)}) collective-permute-start(f32[2,2,4,128,128]{4,3,2,1,0:T(8,128)} %get-tuple-element.35), channel_id=1, source_target_pairs={{0,16},{16,32},{32,48},{48,64},{64,80},{80,96},{96,112},{112,128},... | collective-permute-start | bytes 3145736 | tf_op jit(solution)/shard_map/ppermute | solution.py:426
  8.1 23.1 %collective-permute-start.9 = (f32[2,1,4,128,128]{4,3,2,1,0:T(8,128)}, f32[2,1,4,128,128]{4,3,2,1,0:T(8,128)S(1)}, u32[]{:S(2)}, u32[]{:S(2)}) collective-permute-start(f32[2,1,4,128,128]{4,3,2,1,0:T(8,128)} %get-tuple-element.36), channel_id=1, source_target_pairs={{16,0},{32,16},{48,32},{64,48},{80,64},{96,80},{112,96},{128,112},... | collective-permute-start | bytes 1572872 | tf_op jit(solution)/shard_map/ppermute | solution.py:427
  11.1 5.7 %collective-permute-start.2 = (f32[120,128]{1,0:T(8,128)S(1)}, f32[120,128]{1,0:T(8,128)S(1)}, u32[]{:S(2)}, u32[]{:S(2)}) collective-permute-start(f32[120,128]{1,0:T(8,128)S(1)} %reshape.11), channel_id=1, source_target_pairs={{3,0},{0,1},{1,2},{2,3},{7,4},{4,5},{5,6},{6,7},{11,8},{8,9},{9,10... | collective-permute-start | bytes 184328 | tf_op jit(solution)/shard_map/ppermute | solution.py:419
  12.6 5.7 %collective-permute-start.3 = (f32[120,128]{1,0:T(8,128)S(1)}, f32[120,128]{1,0:T(8,128)S(1)}, u32[]{:S(2)}, u32[]{:S(2)}) collective-permute-start(f32[120,128]{1,0:T(8,128)S(1)} %reshape.11), channel_id=1, source_target_pairs={{2,0},{3,1},{0,2},{1,3},{6,4},{7,5},{4,6},{5,7},{10,8},{11,9},{8,1... | collective-permute-start | bytes 184328 | tf_op jit(solution)/shard_map/ppermute | solution.py:419
  15.4 4.6 %collective-permute-start.4 = (f32[120,128]{1,0:T(8,128)S(1)}, f32[120,128]{1,0:T(8,128)S(1)}, u32[]{:S(2)}, u32[]{:S(2)}) collective-permute-start(f32[120,128]{1,0:T(8,128)S(1)} %reshape.11), channel_id=1, source_target_pairs={{1,0},{2,1},{3,2},{0,3},{5,4},{6,5},{7,6},{4,7},{9,8},{10,9},{11,1... | collective-permute-start | bytes 184328 | tf_op jit(solution)/shard_map/ppermute | solution.py:419
  20.0 11.1 %copy-start = (f32[64,128]{1,0:T(8,128)S(1)}, f32[64,128]{1,0:T(8,128)}, u32[]{:S(2)}) copy-start(f32[64,128]{1,0:T(8,128)} %get-tuple-element.38.bias_ref) | copy-start | bytes 98308
  20.0 11.1 %copy-start.1 = (f32[64,128]{1,0:T(8,128)S(1)}, f32[64,128]{1,0:T(8,128)}, u32[]{:S(2)}) copy-start(f32[64,128]{1,0:T(8,128)} %get-tuple-element.39.rate_ref) | copy-start | bytes 98308
  20.0 11.1 %copy-start.2 = (bf16[128,128]{1,0:T(8,128)(2,1)S(1)}, bf16[128,128]{1,0:T(8,128)(2,1)}, u32[]{:S(2)}) copy-start(bf16[128,128]{1,0:T(8,128)(2,1)} %get-tuple-element.37.mixing_ref) | copy-start | bytes 98308
  20.1 11.1 %copy-start.3 = (s32[24,4]{0,1:T(4,128)S(1)}, s32[24,4]{0,1:T(4,128)}, u32[]{:S(2)}) copy-start(s32[24,4]{0,1:T(4,128)} %param.13) | copy-start | bytes 1156
  20.1 11.1 %copy-start.5 = (s32[24]{0:T(128)S(1)}, s32[24]{0:T(128)}, u32[]{:S(2)}) copy-start(s32[24]{0:T(128)} %count_ref.7) | copy-start | bytes 292
  20.1 11.1 %copy-start.6 = (s32[2]{0:T(128)S(1)}, s32[2]{0:T(128)}, u32[]{:S(2)}) copy-start(s32[2]{0:T(128)} %month_ref.5) | copy-start | bytes 28
  20.1 11.1 %copy-start.7 = (s32[2]{0:T(128)S(1)}, s32[2]{0:T(128)}, u32[]{:S(2)}) copy-start(s32[2]{0:T(128)} %weight_ref.5) | copy-start | bytes 28
  20.1 8.9 %collective-permute-start.5 = (f32[480,128]{1,0:T(8,128)S(1)}, f32[480,128]{1,0:T(8,128)S(1)}, u32[]{:S(2)}, u32[]{:S(2)}) collective-permute-start(f32[480,128]{1,0:T(8,128)S(1)} %pad_maximum_fusion.near_ref), channel_id=1, source_target_pairs={{12,0},{13,1},{14,2},{15,3},{0,4},{1,5},{2,6},{3,7},{4,8},{5,9},{6... | collective-permute-start | bytes 737288 | tf_op jit(solution)/shard_map/ppermute | solution.py:424
  21.0 8.0 %collective-permute-start.6 = (f32[480,128]{1,0:T(8,128)S(1)}, f32[480,128]{1,0:T(8,128)S(1)}, u32[]{:S(2)}, u32[]{:S(2)}) collective-permute-start(f32[480,128]{1,0:T(8,128)S(1)} %pad_maximum_fusion.near_ref), channel_id=1, source_target_pairs={{8,0},{9,1},{10,2},{11,3},{12,4},{13,5},{14,6},{15,7},{0,8},{1,9},... | collective-permute-start | bytes 737288 | tf_op jit(solution)/shard_map/ppermute | solution.py:424
  21.9 9.2 %collective-permute-start.7 = (f32[480,128]{1,0:T(8,128)S(1)}, f32[480,128]{1,0:T(8,128)S(1)}, u32[]{:S(2)}, u32[]{:S(2)}) collective-permute-start(f32[480,128]{1,0:T(8,128)S(1)} %pad_maximum_fusion.near_ref), channel_id=1, source_target_pairs={{4,0},{5,1},{6,2},{7,3},{8,4},{9,5},{10,6},{11,7},{12,8},{13,9},{1... | collective-permute-start | bytes 737288 | tf_op jit(solution)/shard_map/ppermute | solution.py:424
  31.2 6.7 %copy-start.4 = (bf16[16,128]{1,0:T(8,128)(2,1)S(1)}, bf16[16,128]{1,0:T(8,128)(2,1)}, u32[]{:S(2)}) copy-start(bf16[16,128]{1,0:T(8,128)(2,1)} %get-tuple-element.43.mixing_ref) | copy-start | bytes 12292
  34.9 6.9 %collective-permute-start.10 = (f32[64,512]{1,0:T(8,128)S(1)}, f32[64,512]{1,0:T(8,128)S(1)}, u32[]{:S(2)}, u32[]{:S(2)}) collective-permute-start(f32[64,512]{1,0:T(8,128)S(1)} %get-tuple-element.40.low_ref), channel_id=1, source_target_pairs={{0,16},{16,32},{32,48},{48,64},{64,80},{80,96},{96,112},{112,128},... | collective-permute-start | bytes 393224 | tf_op jit(solution)/shard_map/ppermute | solution.py:449
  34.9 6.9 %collective-permute-start.11 = (f32[64,256]{1,0:T(8,128)S(1)}, f32[64,256]{1,0:T(8,128)S(1)}, u32[]{:S(2)}, u32[]{:S(2)}) collective-permute-start(f32[64,256]{1,0:T(8,128)S(1)} %get-tuple-element.41.high_ref), channel_id=1, source_target_pairs={{16,0},{32,16},{48,32},{64,48},{80,64},{96,80},{112,96},{128,112},... | collective-permute-start | bytes 196616 | tf_op jit(solution)/shard_map/ppermute | solution.py:450

commit v5 on v4

--- a/solution.py
+++ b/solution.py
@@ -69,6 +69,18 @@
         axis=0,
     )
     product = lax.dot_general(left, right, NT, preferred_element_type=F32)
+    return combine(product, coef, half)
+
+
+def tile_row(values_ref, tiles_ref, tables, row, coef, half):
+    width = tables[2].shape[0]
+    spare = tiles_ref.shape[0] + LOW + HIGH
+    left = jnp.concatenate(
+        [values_ref[column(*tables, row, r, spare)] for r in range(width)], axis=1
+    )
+    product = lax.dot_general(
+        left, tiles_ref[row], (((1,), (0,)), ((), ())), preferred_element_type=F32
+    )
     return combine(product, coef, half)
 
 
@@ -192,13 +204,16 @@
     )(*scalars, explicit_blocks, explicit_blocks, *source)
 
 
-def load_kernel(explicit_ref, implicit_ref, explicit_out_ref, implicit_out_ref, sems):
+def load_kernel(
+    explicit_ref, implicit_ref, tiles_ref, implicit_out_ref, explicit_here_ref, sems
+):
     chunks = sems.shape[1]
+    _, rows, width, block, _ = explicit_ref.shape
+    step = rows // chunks
     copies = []
     for k, (source, target) in enumerate(
-        ((explicit_ref, explicit_out_ref), (implicit_ref, implicit_out_ref))
+        ((explicit_ref, explicit_here_ref), (implicit_ref, implicit_out_ref))
     ):
-        step = source.shape[1] // chunks
         for c in range(chunks):
             at = pl.ds(c * step, step)
             copies.append(
@@ -206,11 +221,24 @@
             )
     for copy in copies:
         copy.start()
-    for copy in copies:
+    for row in range(rows):
+        if row % step == 0:
+            copies[row // step].wait()
+        for r in range(0, width, 2):
+            both = jnp.concatenate(
+                [
+                    jnp.concatenate([explicit_here_ref[m, row, r + k] for k in range(2)], axis=1)
+                    for m in range(2)
+                ],
+                axis=0,
+            )
+            tiles_ref[row, r * block : (r + 2) * block, :] = both.T
+    for copy in copies[chunks:]:
         copy.wait()
 
 
 def load(explicit_blocks, implicit_blocks):
+    months, rows, width, block, _ = explicit_blocks.shape
     hbm = pl.BlockSpec(memory_space=pl.ANY)
     vmem = pl.BlockSpec(memory_space=pltpu.VMEM)
     return pl.pallas_call(
@@ -218,10 +246,13 @@
         in_specs=[hbm, hbm],
         out_specs=[vmem, vmem],
         out_shape=[
+            pltpu.VMEM((rows, width * block, months * block), explicit_blocks.dtype),
+            pltpu.VMEM(implicit_blocks.shape, implicit_blocks.dtype),
+        ],
+        scratch_shapes=[
             pltpu.VMEM(explicit_blocks.shape, explicit_blocks.dtype),
-            pltpu.VMEM(implicit_blocks.shape, implicit_blocks.dtype),
-        ],
-        scratch_shapes=[pltpu.SemaphoreType.DMA((2, 4))],
+            pltpu.SemaphoreType.DMA((2, 6)),
+        ],
         compiler_params=pltpu.CompilerParams(vmem_limit_bytes=44 * MIB),
         cost_estimate=pl.CostEstimate(flops=0, bytes_accessed=24 * MIB, transcendentals=0),
         name="load",
@@ -235,8 +266,8 @@
 ):
     coef = coefficients(month_ref, weight_ref, 0)
     tables = (total, origin_ref, cols_ref, count_ref)
-    rows = explicit_ref.shape[1]
-    block = explicit_ref.shape[-1]
+    rows = implicit_ref.shape[1]
+    block = implicit_ref.shape[-1]
     tracers = bias_ref.shape[0]
     ext = rows + LOW + HIGH
     share = near_ref.shape[0] // ext
@@ -260,7 +291,7 @@
         frame = rows + REACH + row
         finish(frame, edge_row(values_ref, right_ref, row, frame, coef, tracers))
     for row in range(rows):
-        finish(row + REACH, own_row(values_ref, explicit_ref, tables, row, 0, coef, tracers))
+        finish(row + REACH, tile_row(values_ref, explicit_ref, tables, row, coef, tracers))
     for at in range(LOW):
         low_ref[:, at * block : (at + 1) * block] = own_row(
             middle_ref, implicit_ref, tables, rows - LOW + at, REACH, coef, tracers
@@ -278,8 +309,8 @@
 ):
     coef = coefficients(month_ref, weight_ref, 0)
     tables = (total, origin_ref, cols_ref, count_ref)
-    rows = explicit_ref.shape[1]
-    block = explicit_ref.shape[-1]
+    rows = implicit_ref.shape[1]
+    block = implicit_ref.shape[-1]
     tracers = low_ref.shape[0]
     mine = bias_ref.shape[0] // (SIDE * SIDE)
     ext = rows + LOW + HIGH
@@ -298,7 +329,7 @@
     coef = coefficients(month_ref, weight_ref, 1)
     mixing, bias, rate = mixing_ref[...], bias_ref[:mine, :], rate_ref[:mine, :]
     for row in range(REACH, rows - REACH + 1):
-        product = own_row(own_ref, explicit_ref, tables, row, 0, coef, mine)
+        product = tile_row(own_ref, explicit_ref, tables, row, coef, mine)
         source = half_source(field_ref[row], mixing, bias, rate)
         own_store(own_middle_ref, row + REACH, product + source)
 
@@ -310,8 +341,8 @@
 ):
     coef = coefficients(month_ref, weight_ref, 1)
     tables = (total, origin_ref, cols_ref, count_ref)
-    rows = explicit_ref.shape[1]
-    block = explicit_ref.shape[-1]
+    rows = implicit_ref.shape[1]
+    block = implicit_ref.shape[-1]
     mine = bias_ref.shape[0] // (SIDE * SIDE)
     ext = rows + LOW + HIGH
     own_ref[LOW : LOW + rows] = own_in_ref[LOW : LOW + rows]
@@ -339,7 +370,7 @@
         product = edge_row(own_ref, right_ref, row, frame, coef, mine)
         finish(frame, halo_ref[LOW + row], product)
     for row in [*range(REACH), *range(rows - REACH + 1, rows)]:
-        product = own_row(own_ref, explicit_ref, tables, row, 0, coef, mine)
+        product = tile_row(own_ref, explicit_ref, tables, row, coef, mine)
         finish(row + REACH, field_ref[row], product)
     for row in range(rows):
         out_ref[:, row * block : (row + 1) * block] = own_row(

time: 45.5 us -> 43.9 us (0.965)
  Pallas kernels: 18.6 us -> 16.9 us
    pallas_call x3, Pallas kernels: 11.2 us -> 9.54 us  [call(): pl.pallas_call(kernel, in_specs=[smem] * smem_count + [hbm] * hbm_count +...]
  transfers between devices with their start and end apart: 12 -> 12, of which waited for: 4 -> 4; matrix products, arithmetic and copies ran while one was open for 0% -> 0% of each run, Pallas kernels for 25% -> 24%
where the time goes in v5:
time: 43.9 us; the launch traced here: 43.8 us
  starting transfers between devices  19.6 us (45%)
  Pallas kernels  16.9 us (38%)
  waiting for transfers between devices  6.91 us (16%)
    pallas_call x3, Pallas kernels, call(): pl.pallas_call(kernel, in_specs=[smem] * smem_count + [hbm] * hbm_count +...  9.54 us
    ppermute x3, starting transfers between devices, per_device(): lax.ppermute(extended, both, along(0, k))  5.73 us
    ppermute x1, starting transfers between devices, per_device(): high = lax.ppermute(tracers, 'pts', backward)[:, :HIGH * block]  5.3 us
    pallas_call x1, Pallas kernels, load(): pl.pallas_call(load_kernel, in_specs=[hbm, hbm], out_specs=[vmem, vmem],...  4.7 us
    ppermute x3, waiting for transfers between devices, per_device(): lax.ppermute(line, both, along(1, k))  3.69 us
    ppermute x3, waiting for transfers between devices, per_device(): lax.ppermute(extended, both, along(0, k))  3.21 us
    ppermute x1, starting transfers between devices, per_device(): right = lax.ppermute(to_left, 'pts', backward)  2.94 us
    ppermute x1, starting transfers between devices, per_device(): high_in = lax.ppermute(high, 'pts', backward)  2.94 us
  transfers between devices with their start and end apart: 12, of which 4 were waited for; matrix products, arithmetic and copies ran while one was open for 0% of the time, Pallas kernels for 24%

profile of v5, /device:TPU:16, one launch (start us, length us, event | category | flops | bytes accessed | tf_op | source)
XLA Modules:
  0.0 43.8 jit_solution(9846902335415055558)
XLA Ops:
  0.0 0.0 collective-permute-start
  0.0 5.3 %collective-permute-start.1 = (f32[4,3072]{1,0:T(4,128)}, f32[4,3072]{1,0:T(4,128)S(1)}, u32[]{:S(2)}, u32[]{:S(2)}) collective-permute-start(f32[4,3072]{1,0:T(4,128)} %param.10), channel_id=1, source_target_pairs={{16,0},{32,16},{48,32},{64,48},{80,64},{96,80},{112,96},{128,112},... | collective-permute-start | bytes 147464 | tf_op jit(solution)/shard_map/ppermute | solution.py:422
  5.3 0.0 copy-start.8
  5.3 2.7 %edges.1 = (f32[2,2,4,128,128]{4,3,2,1,0:T(8,128)}, f32[2,1,4,128,128]{4,3,2,1,0:T(8,128)}, bf16[128,128]{1,0:T(8,128)(2,1)}, bf16[16,128]{1,0:T(8,128)(2,1)}, f32[64,128]{1,0:T(8,128)}, /*index=5*/f32[64,128]{1,0:T(8,128)}) custom-call(s32[1]{0:T(128)} %bitcast.origin_ref, s32[1]{0:T(128)} %bitcast.2.place_ref, s32[4,24]{1,0:T(4,128)} %bitcast.5, ...), custom_call_target="tpu_custom_call" | custom-call | tf_op jit(solution)/shard_map/edges/pallas_call | solution.py:187
  8.0 0.0 collective-permute-done
  8.0 0.0 collective-permute-done.1
  8.0 0.0 collective-permute-start.8
  8.1 2.9 %collective-permute-start.9 = (f32[2,1,4,128,128]{4,3,2,1,0:T(8,128)}, f32[2,1,4,128,128]{4,3,2,1,0:T(8,128)S(1)}, u32[]{:S(2)}, u32[]{:S(2)}) collective-permute-start(f32[2,1,4,128,128]{4,3,2,1,0:T(8,128)} %get-tuple-element.36), channel_id=1, source_target_pairs={{16,0},{32,16},{48,32},{64,48},{80,64},{96,80},{112,96},{128,112},... | collective-permute-start | bytes 1572872 | tf_op jit(solution)/shard_map/ppermute | solution.py:458
  11.0 0.0 copy-done.8
  11.1 1.6 %collective-permute-start.2 = (f32[120,128]{1,0:T(8,128)S(1)}, f32[120,128]{1,0:T(8,128)S(1)}, u32[]{:S(2)}, u32[]{:S(2)}) collective-permute-start(f32[120,128]{1,0:T(8,128)S(1)} %reshape.11), channel_id=1, source_target_pairs={{3,0},{0,1},{1,2},{2,3},{7,4},{4,5},{5,6},{6,7},{11,8},{8,9},{9,10... | collective-permute-start | bytes 184328 | tf_op jit(solution)/shard_map/ppermute | solution.py:450
  12.6 2.7 %collective-permute-start.3 = (f32[120,128]{1,0:T(8,128)S(1)}, f32[120,128]{1,0:T(8,128)S(1)}, u32[]{:S(2)}, u32[]{:S(2)}) collective-permute-start(f32[120,128]{1,0:T(8,128)S(1)} %reshape.11), channel_id=1, source_target_pairs={{2,0},{3,1},{0,2},{1,3},{6,4},{7,5},{4,6},{5,7},{10,8},{11,9},{8,1... | collective-permute-start | bytes 184328 | tf_op jit(solution)/shard_map/ppermute | solution.py:450
  15.4 1.4 %collective-permute-start.4 = (f32[120,128]{1,0:T(8,128)S(1)}, f32[120,128]{1,0:T(8,128)S(1)}, u32[]{:S(2)}, u32[]{:S(2)}) collective-permute-start(f32[120,128]{1,0:T(8,128)S(1)} %reshape.11), channel_id=1, source_target_pairs={{1,0},{2,1},{3,2},{0,3},{5,4},{6,5},{7,6},{4,7},{9,8},{10,9},{11,1... | collective-permute-start | bytes 184328 | tf_op jit(solution)/shard_map/ppermute | solution.py:450
  16.8 0.0 collective-permute-done.2
  16.8 1.6 %collective-permute-done.3 = f32[120,128]{1,0:T(8,128)S(1)} collective-permute-done((f32[120,128]{1,0:T(8,128)S(1)}, f32[120,128]{1,0:T(8,128)S(1)}, u32[]{:S(2)}, u32[]{:S(2)}) %collective-permute-start.3) | collective-permute-done | bytes 61472 | tf_op jit(solution)/shard_map/ppermute | solution.py:450
  18.4 1.6 %collective-permute-done.4 = f32[120,128]{1,0:T(8,128)S(1)} collective-permute-done((f32[120,128]{1,0:T(8,128)S(1)}, f32[120,128]{1,0:T(8,128)S(1)}, u32[]{:S(2)}, u32[]{:S(2)}) %collective-permute-start.4) | collective-permute-done | bytes 61472 | tf_op jit(solution)/shard_map/ppermute | solution.py:450
  20.0 0.0 copy-start
  20.0 0.0 copy-start.1
  20.0 0.0 copy-start.2
  20.1 0.0 copy-start.3
  20.1 0.0 copy-start.5
  20.1 0.0 copy-start.6
  20.1 0.0 copy-start.7
  20.1 0.9 %collective-permute-start.5 = (f32[480,128]{1,0:T(8,128)S(1)}, f32[480,128]{1,0:T(8,128)S(1)}, u32[]{:S(2)}, u32[]{:S(2)}) collective-permute-start(f32[480,128]{1,0:T(8,128)S(1)} %pad_maximum_fusion.near_ref), channel_id=1, source_target_pairs={{12,0},{13,1},{14,2},{15,3},{0,4},{1,5},{2,6},{3,7},{4,8},{5,9},{6... | collective-permute-start | bytes 737288 | tf_op jit(solution)/shard_map/ppermute | solution.py:455
  21.0 0.8 %collective-permute-start.6 = (f32[480,128]{1,0:T(8,128)S(1)}, f32[480,128]{1,0:T(8,128)S(1)}, u32[]{:S(2)}, u32[]{:S(2)}) collective-permute-start(f32[480,128]{1,0:T(8,128)S(1)} %pad_maximum_fusion.near_ref), channel_id=1, source_target_pairs={{8,0},{9,1},{10,2},{11,3},{12,4},{13,5},{14,6},{15,7},{0,8},{1,9},... | collective-permute-start | bytes 737288 | tf_op jit(solution)/shard_map/ppermute | solution.py:455
  21.9 0.9 %collective-permute-start.7 = (f32[480,128]{1,0:T(8,128)S(1)}, f32[480,128]{1,0:T(8,128)S(1)}, u32[]{:S(2)}, u32[]{:S(2)}) collective-permute-start(f32[480,128]{1,0:T(8,128)S(1)} %pad_maximum_fusion.near_ref), channel_id=1, source_target_pairs={{4,0},{5,1},{6,2},{7,3},{8,4},{9,5},{10,6},{11,7},{12,8},{13,9},{1... | collective-permute-start | bytes 737288 | tf_op jit(solution)/shard_map/ppermute | solution.py:455
  22.7 4.7 %load.1 = (bf16[24,512,256]{2,1,0:T(8,128)(2,1)S(1)}, bf16[2,24,4,128,128]{4,3,2,1,0:T(8,128)(2,1)S(1)}) custom-call(bf16[2,24,4,128,128]{4,3,2,1,0:T(8,128)(2,1)} %explicit_ref, bf16[2,24,4,128,128]{4,3,2,1,0:T(8,128)(2,1)} %implicit_ref), custom_call_target="tpu_custom_call" | custom-call | bytes 25165824 | tf_op jit(solution)/shard_map/load/pallas_call | solution.py:244
  27.4 1.6 %collective-permute-done.5.next_ref = f32[480,128]{1,0:T(8,128)S(1)} collective-permute-done((f32[480,128]{1,0:T(8,128)S(1)}, f32[480,128]{1,0:T(8,128)S(1)}, u32[]{:S(2)}, u32[]{:S(2)}) %collective-permute-start.5) | collective-permute-done | bytes 245792 | tf_op jit(solution)/shard_map/ppermute | solution.py:455
  29.0 0.0 collective-permute-done.6.far_ref
  29.0 2.1 %collective-permute-done.7.back_ref = f32[480,128]{1,0:T(8,128)S(1)} collective-permute-done((f32[480,128]{1,0:T(8,128)S(1)}, f32[480,128]{1,0:T(8,128)S(1)}, u32[]{:S(2)}, u32[]{:S(2)}) %collective-permute-start.7) | collective-permute-done | bytes 245792 | tf_op jit(solution)/shard_map/ppermute | solution.py:455
  31.1 0.0 collective-permute-done.9.right_ref
  31.1 0.0 collective-permute-done.8.left_ref
  31.1 0.0 copy-done
  31.1 0.0 copy-done.1
  31.1 0.0 copy-done.2
  31.2 0.0 copy-done.3
  31.2 0.0 copy-done.5
  31.2 0.0 copy-done.6
  31.2 0.0 copy-done.7
  31.2 0.0 copy-start.4
  31.2 2.9 %first.1 = (f32[64,512]{1,0:T(8,128)S(1)}, f32[64,256]{1,0:T(8,128)S(1)}, bf16[29,128,128]{2,1,0:T(8,128)(2,1)S(1)}) custom-call(s32[1]{0:T(128)} %bitcast.origin_ref, s32[4,24]{1,0:T(4,128)S(1)} %bitcast.6, s32[24]{0:T(128)S(1)} %copy-done.5, s32[2]{0:T(128)S(1)} %copy-done.6, s32[2]{0:T(128)S(1)} %copy-done.7, ...), custom_call_target="tpu_custom_call" | custom-call | flops 1107296256 | bytes 8388608 | tf_op jit(solution)/shard_map/first/pallas_call | solution.py:385
  34.1 0.0 collective-permute-start.10
  34.1 2.9 %collective-permute-start.11 = (f32[64,256]{1,0:T(8,128)S(1)}, f32[64,256]{1,0:T(8,128)S(1)}, u32[]{:S(2)}, u32[]{:S(2)}) collective-permute-start(f32[64,256]{1,0:T(8,128)S(1)} %get-tuple-element.41.high_ref), channel_id=1, source_target_pairs={{16,0},{32,16},{48,32},{64,48},{80,64},{96,80},{112,96},{128,112},... | collective-permute-start | bytes 196616 | tf_op jit(solution)/shard_map/ppermute | solution.py:481
  37.1 0.0 copy-done.4
  37.1 3.2 %inner.1 = (bf16[24,128,128]{2,1,0:T(8,128)(2,1)S(1)}, bf16[31,16,128]{2,1,0:T(8,128)(2,1)S(1)}, bf16[29,16,128]{2,1,0:T(8,128)(2,1)S(1)}) custom-call(s32[1]{0:T(128)} %bitcast.origin_ref, s32[4,24]{1,0:T(4,128)S(1)} %bitcast.7, s32[24]{0:T(128)S(1)} %copy-done.5, s32[2]{0:T(128)S(1)} %copy-done.6, s32[2]{0:T(128)S(1)} %copy-done.7, ...), custom_call_target="tpu_custom_call" | custom-call | flops 1308622848 | bytes 8388608 | tf_op jit(solution)/shard_map/inner/pallas_call | solution.py:385
  40.3 0.0 collective-permute-done.11.high_in_ref
  40.3 0.0 collective-permute-done.10.low_in_ref
  40.3 3.4 %last.1 = f32[4,3072]{1,0:T(4,128)} custom-call(s32[1]{0:T(128)} %bitcast.origin_ref, s32[4,24]{1,0:T(4,128)S(1)} %bitcast.8, s32[24]{0:T(128)S(1)} %copy-done.5, s32[2]{0:T(128)S(1)} %copy-done.6, s32[2]{0:T(128)S(1)} %copy-done.7, f32[64,512]{1,0:T(8,128)S(1)} %collective-permute-done.10.low_in_ref, f32[64,256]{1,0:T(8,128)S(1)} %collective-permute-done.11.high_in_ref, ...), custom_call_target="tpu_custom_call" | custom-call | flops 1006632960 | bytes 8388608 | tf_op jit(solution)/shard_map/last/pallas_call | solution.py:385
  (5 shorter events, 0.1 us)
Async XLA Ops:
  0.0 8.0 %collective-permute-start = (f32[4,3072]{1,0:T(4,128)}, f32[4,3072]{1,0:T(4,128)S(1)}, u32[]{:S(2)}, u32[]{:S(2)}) collective-permute-start(f32[4,3072]{1,0:T(4,128)} %param.10), channel_id=1, source_target_pairs={{0,16},{16,32},{32,48},{48,64},{64,80},{80,96},{96,112},{112,128},... | collective-permute-start | bytes 147464 | tf_op jit(solution)/shard_map/ppermute | solution.py:421
  0.0 8.0 %collective-permute-start.1 = (f32[4,3072]{1,0:T(4,128)}, f32[4,3072]{1,0:T(4,128)S(1)}, u32[]{:S(2)}, u32[]{:S(2)}) collective-permute-start(f32[4,3072]{1,0:T(4,128)} %param.10), channel_id=1, source_target_pairs={{16,0},{32,16},{48,32},{64,48},{80,64},{96,80},{112,96},{128,112},... | collective-permute-start | bytes 147464 | tf_op jit(solution)/shard_map/ppermute | solution.py:422
  5.3 5.7 %copy-start.8 = (f32[4,3072]{1,0:T(4,128)S(1)}, f32[4,3072]{1,0:T(4,128)}, u32[]{:S(2)}) copy-start(f32[4,3072]{1,0:T(4,128)} %param.10) | copy-start | bytes 147460
  8.0 23.1 %collective-permute-start.8 = (f32[2,2,4,128,128]{4,3,2,1,0:T(8,128)}, f32[2,2,4,128,128]{4,3,2,1,0:T(8,128)S(1)}, u32[]{:S(2)}, u32[]{:S(2)}) collective-permute-start(f32[2,2,4,128,128]{4,3,2,1,0:T(8,128)} %get-tuple-element.35), channel_id=1, source_target_pairs={{0,16},{16,32},{32,48},{48,64},{64,80},{80,96},{96,112},{112,128},... | collective-permute-start | bytes 3145736 | tf_op jit(solution)/shard_map/ppermute | solution.py:457
  8.1 23.1 %collective-permute-start.9 = (f32[2,1,4,128,128]{4,3,2,1,0:T(8,128)}, f32[2,1,4,128,128]{4,3,2,1,0:T(8,128)S(1)}, u32[]{:S(2)}, u32[]{:S(2)}) collective-permute-start(f32[2,1,4,128,128]{4,3,2,1,0:T(8,128)} %get-tuple-element.36), channel_id=1, source_target_pairs={{16,0},{32,16},{48,32},{64,48},{80,64},{96,80},{112,96},{128,112},... | collective-permute-start | bytes 1572872 | tf_op jit(solution)/shard_map/ppermute | solution.py:458
  11.1 5.7 %collective-permute-start.2 = (f32[120,128]{1,0:T(8,128)S(1)}, f32[120,128]{1,0:T(8,128)S(1)}, u32[]{:S(2)}, u32[]{:S(2)}) collective-permute-start(f32[120,128]{1,0:T(8,128)S(1)} %reshape.11), channel_id=1, source_target_pairs={{3,0},{0,1},{1,2},{2,3},{7,4},{4,5},{5,6},{6,7},{11,8},{8,9},{9,10... | collective-permute-start | bytes 184328 | tf_op jit(solution)/shard_map/ppermute | solution.py:450
  12.6 5.7 %collective-permute-start.3 = (f32[120,128]{1,0:T(8,128)S(1)}, f32[120,128]{1,0:T(8,128)S(1)}, u32[]{:S(2)}, u32[]{:S(2)}) collective-permute-start(f32[120,128]{1,0:T(8,128)S(1)} %reshape.11), channel_id=1, source_target_pairs={{2,0},{3,1},{0,2},{1,3},{6,4},{7,5},{4,6},{5,7},{10,8},{11,9},{8,1... | collective-permute-start | bytes 184328 | tf_op jit(solution)/shard_map/ppermute | solution.py:450
  15.4 4.6 %collective-permute-start.4 = (f32[120,128]{1,0:T(8,128)S(1)}, f32[120,128]{1,0:T(8,128)S(1)}, u32[]{:S(2)}, u32[]{:S(2)}) collective-permute-start(f32[120,128]{1,0:T(8,128)S(1)} %reshape.11), channel_id=1, source_target_pairs={{1,0},{2,1},{3,2},{0,3},{5,4},{6,5},{7,6},{4,7},{9,8},{10,9},{11,1... | collective-permute-start | bytes 184328 | tf_op jit(solution)/shard_map/ppermute | solution.py:450
  20.0 11.1 %copy-start = (f32[64,128]{1,0:T(8,128)S(1)}, f32[64,128]{1,0:T(8,128)}, u32[]{:S(2)}) copy-start(f32[64,128]{1,0:T(8,128)} %get-tuple-element.38.bias_ref) | copy-start | bytes 98308
  20.0 11.1 %copy-start.1 = (f32[64,128]{1,0:T(8,128)S(1)}, f32[64,128]{1,0:T(8,128)}, u32[]{:S(2)}) copy-start(f32[64,128]{1,0:T(8,128)} %get-tuple-element.39.rate_ref) | copy-start | bytes 98308
  20.0 11.1 %copy-start.2 = (bf16[128,128]{1,0:T(8,128)(2,1)S(1)}, bf16[128,128]{1,0:T(8,128)(2,1)}, u32[]{:S(2)}) copy-start(bf16[128,128]{1,0:T(8,128)(2,1)} %get-tuple-element.37.mixing_ref) | copy-start | bytes 98308
  20.1 11.1 %copy-start.3 = (s32[24,4]{0,1:T(4,128)S(1)}, s32[24,4]{0,1:T(4,128)}, u32[]{:S(2)}) copy-start(s32[24,4]{0,1:T(4,128)} %param.13) | copy-start | bytes 1156
  20.1 11.1 %copy-start.5 = (s32[24]{0:T(128)S(1)}, s32[24]{0:T(128)}, u32[]{:S(2)}) copy-start(s32[24]{0:T(128)} %count_ref.7) | copy-start | bytes 292
  20.1 11.1 %copy-start.6 = (s32[2]{0:T(128)S(1)}, s32[2]{0:T(128)}, u32[]{:S(2)}) copy-start(s32[2]{0:T(128)} %month_ref.5) | copy-start | bytes 28
  20.1 11.1 %copy-start.7 = (s32[2]{0:T(128)S(1)}, s32[2]{0:T(128)}, u32[]{:S(2)}) copy-start(s32[2]{0:T(128)} %weight_ref.5) | copy-start | bytes 28
  20.1 8.9 %collective-permute-start.5 = (f32[480,128]{1,0:T(8,128)S(1)}, f32[480,128]{1,0:T(8,128)S(1)}, u32[]{:S(2)}, u32[]{:S(2)}) collective-permute-start(f32[480,128]{1,0:T(8,128)S(1)} %pad_maximum_fusion.near_ref), channel_id=1, source_target_pairs={{12,0},{13,1},{14,2},{15,3},{0,4},{1,5},{2,6},{3,7},{4,8},{5,9},{6... | collective-permute-start | bytes 737288 | tf_op jit(solution)/shard_map/ppermute | solution.py:455
  21.0 8.0 %collective-permute-start.6 = (f32[480,128]{1,0:T(8,128)S(1)}, f32[480,128]{1,0:T(8,128)S(1)}, u32[]{:S(2)}, u32[]{:S(2)}) collective-permute-start(f32[480,128]{1,0:T(8,128)S(1)} %pad_maximum_fusion.near_ref), channel_id=1, source_target_pairs={{8,0},{9,1},{10,2},{11,3},{12,4},{13,5},{14,6},{15,7},{0,8},{1,9},... | collective-permute-start | bytes 737288 | tf_op jit(solution)/shard_map/ppermute | solution.py:455
  21.9 9.2 %collective-permute-start.7 = (f32[480,128]{1,0:T(8,128)S(1)}, f32[480,128]{1,0:T(8,128)S(1)}, u32[]{:S(2)}, u32[]{:S(2)}) collective-permute-start(f32[480,128]{1,0:T(8,128)S(1)} %pad_maximum_fusion.near_ref), channel_id=1, source_target_pairs={{4,0},{5,1},{6,2},{7,3},{8,4},{9,5},{10,6},{11,7},{12,8},{13,9},{1... | collective-permute-start | bytes 737288 | tf_op jit(solution)/shard_map/ppermute | solution.py:455
  31.2 5.9 %copy-start.4 = (bf16[16,128]{1,0:T(8,128)(2,1)S(1)}, bf16[16,128]{1,0:T(8,128)(2,1)}, u32[]{:S(2)}) copy-start(bf16[16,128]{1,0:T(8,128)(2,1)} %get-tuple-element.43.mixing_ref) | copy-start | bytes 12292
  34.1 6.2 %collective-permute-start.10 = (f32[64,512]{1,0:T(8,128)S(1)}, f32[64,512]{1,0:T(8,128)S(1)}, u32[]{:S(2)}, u32[]{:S(2)}) collective-permute-start(f32[64,512]{1,0:T(8,128)S(1)} %get-tuple-element.40.low_ref), channel_id=1, source_target_pairs={{0,16},{16,32},{32,48},{48,64},{64,80},{80,96},{96,112},{112,128},... | collective-permute-start | bytes 393224 | tf_op jit(solution)/shard_map/ppermute | solution.py:480
  34.1 6.2 %collective-permute-start.11 = (f32[64,256]{1,0:T(8,128)S(1)}, f32[64,256]{1,0:T(8,128)S(1)}, u32[]{:S(2)}, u32[]{:S(2)}) collective-permute-start(f32[64,256]{1,0:T(8,128)S(1)} %get-tuple-element.41.high_ref), channel_id=1, source_target_pairs={{16,0},{32,16},{48,32},{64,48},{80,64},{96,80},{112,96},{128,112},... | collective-permute-start | bytes 196616 | tf_op jit(solution)/shard_map/ppermute | solution.py:481
